TPU v7x, 32 devices: a whole 2x2x4 slice. The times are simulated.
32 devices in a mesh: member: 4 (over x, core), lat: 4 (over z), lon: 2 (over y).
Axes of the slice: x: 2, y: 2, z: 4, core: 2. Of those that a mesh axis runs over, the one named last changes fastest.
Arguments:
- analysis: bfloat16 [96, 16, 256], P('lat', 'lon', 'member'), may hold values from -6 to 6
- noise: bfloat16 [4, 96, 16, 256], P('member', 'lat', 'lon'), may hold values from -6 to 6
- w_in: bfloat16 [256, 256], replicated, may hold values from -0.375 to 0.375
- lat_offsets: int32 [96, 9], P('lat'), may hold values from -1 to 1, as said below
- lon_offsets: int32 [96, 9], P('lat'), may hold values from -8 to 8, as said below
- psi: float32 [96, 9, 3], P('lat'), may hold values from -2 to 2
- w_disco: bfloat16 [3, 256, 256], replicated, may hold values from -0.21875 to 0.21875
- norm_gain: float32 [256], replicated, may hold values from 0.1 to 1.9
- w_up: bfloat16 [256, 512], replicated, may hold values from -0.375 to 0.375
- bias_up: float32 [512], replicated, may hold values from -4 to 4
- w_down: bfloat16 [512, 256], replicated, may hold values from -0.25 to 0.25
Outputs:
- states: bfloat16 [4, 96, 16, 256], P('member', 'lat', 'lon')
Inputs may be any that keep to these rules, and one draw needn't show every extreme that they name: `lat_offsets`: columns 0 and 1 of every row are -1 and +1; the others lie in -1 to 1. `lon_offsets`: at row i with r = min(i, 95 - i), every offset has magnitude at most s = max(1, 8 - (8 * r) // max(24, 1)), and column 2 equals s or -s; row 0 holds 8 and row 95 holds -8.
All inputs are finite; a program needn't handle non-finite values.
Results may differ from a plain program's by a relative error of at most 0.02.
Values may be sent and summed in bfloat16 or wider, within the bound.
No kernel may reach another device: no remote copies, remote signals or barrier semaphores. Data moves between devices by JAX's collectives and lax.ppermute only.
A program may use at most 64 MiB of HBM per device.

v0:
```python
import jax
import jax.numpy as jnp
from jax import lax
from jax.sharding import PartitionSpec as P

B = 3
HW = 8
PASSES = 2


def padded(cells, sides, width, closed):
    for axis, dim in sides:
        count = lax.axis_size(axis)
        ends = count if closed else count - 1
        head = lax.slice_in_dim(cells, 0, width, axis=dim)
        tail = lax.slice_in_dim(cells, cells.shape[dim] - width, cells.shape[dim], axis=dim)
        cells = jnp.concatenate(
            [
                lax.ppermute(tail, axis, [(i, (i + 1) % count) for i in range(ends)]),
                cells,
                lax.ppermute(head, axis, [((i + 1) % count, i) for i in range(ends)]),
            ],
            axis=dim,
        )
    return cells


def passed_along(block, axis, distance):
    devices = range(lax.axis_size(axis))
    route = [((i - distance) % len(devices), i) for i in devices]
    return lax.ppermute(block, axis, route)


def fix_poles(rows, flipped):
    band = lax.axis_index("lat")
    last_band = lax.axis_size("lat") - 1
    top = jnp.where(band == 0, flipped[0], rows[0])
    bottom = jnp.where(band == last_band, flipped[1], rows[-1])
    return jnp.concatenate([top[None], rows[1:-1], bottom[None]], axis=0)


def extend(state):
    half = lax.axis_size("lon") // 2
    rows = padded(state, (("lat", 0),), 1, False)
    edges = jnp.stack([state[0], state[-1]])
    flipped = passed_along(edges, "lon", half)
    rows = fix_poles(rows, flipped)
    return padded(rows, (("lon", 1),), HW, True)


def one_pass(state, lat_offsets, lon_offsets, psi, w_disco, norm_gain, w_up, bias_up, w_down):
    row_count, col_count, width = state.shape
    extended = extend(state)
    span = col_count + 2 * HW
    stacked = jnp.concatenate(
        [extended[0:row_count], extended[1 : row_count + 1], extended[2 : row_count + 2]], axis=1
    )
    row_pick = (
        (lat_offsets + 1)[:, :, None] == jnp.arange(3, dtype=jnp.int32)[None, None, :]
    ).astype(jnp.float32)
    target = jnp.arange(col_count, dtype=jnp.int32)[None, None, :] + HW + lon_offsets[:, :, None]
    col_pick = (
        target[:, :, :, None] == jnp.arange(span, dtype=jnp.int32)[None, None, None, :]
    ).astype(jnp.float32)
    weights = jnp.einsum(
        "ikb,ikr,ikjq->bijrq", psi, row_pick, col_pick, precision=lax.Precision.HIGHEST
    )
    weights = weights.reshape(B, row_count, col_count, 3 * span)
    mix = jnp.einsum(
        "bijp,ipc->bijc", weights, stacked.astype(jnp.float32), precision=lax.Precision.HIGHEST
    )
    mix = mix.astype(jnp.bfloat16)
    inner = state.astype(jnp.float32).reshape(-1, width)
    for basis in range(B):
        inner = inner + jnp.dot(
            mix[basis].reshape(-1, width), w_disco[basis], preferred_element_type=jnp.float32
        )
    mean = jnp.mean(inner, axis=1, keepdims=True)
    centred = inner - mean
    variance = jnp.mean(centred * centred, axis=1, keepdims=True)
    normed = (centred * lax.rsqrt(variance + 1e-05) * norm_gain).astype(jnp.bfloat16)
    hidden = jax.nn.gelu(
        jnp.dot(normed, w_up, preferred_element_type=jnp.float32) + bias_up
    ).astype(jnp.bfloat16)
    result = inner + jnp.dot(hidden, w_down, preferred_element_type=jnp.float32)
    return result.astype(jnp.bfloat16).reshape(row_count, col_count, width)


def shards(
    analysis, noise, w_in, lat_offsets, lon_offsets, psi, w_disco, norm_gain, w_up, bias_up, w_down
):
    row_count, col_count, quarter = analysis.shape
    width = w_in.shape[1]
    start = lax.axis_index("member") * quarter
    own_rows = lax.dynamic_slice_in_dim(w_in, start, quarter, 0)
    partial_base = jnp.dot(
        analysis.reshape(-1, quarter), own_rows, preferred_element_type=jnp.float32
    )
    base = lax.psum(partial_base.astype(jnp.bfloat16), "member").astype(jnp.float32)
    state = (base + noise[0].reshape(-1, width).astype(jnp.float32)).astype(jnp.bfloat16)
    state = state.reshape(row_count, col_count, width)
    for step in range(PASSES):
        state = one_pass(
            state, lat_offsets, lon_offsets, psi, w_disco, norm_gain, w_up, bias_up, w_down
        )
    return state[None]


def solution(mesh):
    return jax.shard_map(
        shards,
        mesh=mesh,
        in_specs=(
            P("lat", "lon", "member"),
            P("member", "lat", "lon", None),
            P(),
            P("lat", None),
            P("lat", None),
            P("lat", None, None),
            P(),
            P(),
            P(),
            P(),
            P(),
        ),
        out_specs=P("member", "lat", "lon", None),
        check_vma=False,
    )
```

profile of v0, /device:TPU:0, one launch (start us, length us, event | category | flops | bytes accessed | tf_op | source)
XLA Modules:
  0.0 88.6 jit_solution(7356655552667442401)
XLA Ops:
  6.5 1.6 %fusion.10 = bf16[192,256]{1,0:T(8,128)(2,1)} fusion(bf16[24,8,64]{2,1,0:T(8,128)(2,1)} %param.11, bf16[256,256]{1,0:T(8,128)(2,1)} %param.13, s32[]{:T(128)S(6)} %select_n.29), kind=kOutput, calls=%fused_computation.21 | convolution fusion | flops 6340608 | bytes 180228 | tf_op jit(solution)/shard_map/dot_general | solution.py:96
  8.2 0.8 copy.17
  9.1 0.7 broadcast_add_fusion.1
  9.9 33.8 %all-reduce.2.cloned.1.call-done = bf16[192,256]{1,0:T(8,128)(2,1)} async-done(((bf16[192,256]{1,0:T(8,128)(2,1)}), bf16[192,256]{1,0:T(8,128)(2,1)}) %all-reduce.2.cloned.1.call-update) | async-done | bytes 98320 | tf_op jit(solution)/shard_map/psum | solution.py:99
  43.7 1.0 %fusion.37 = bf16[192,256]{1,0:T(8,128)(2,1)S(1)} fusion(bf16[192,256]{1,0:T(8,128)(2,1)} %all-reduce.2.cloned.1.call-done, bf16[1,24,8,256]{3,2,1,0:T(8,128)(2,1)} %param.12), kind=kLoop, calls=%fused_computation.55 | loop fusion | flops 196608 | bytes 294912 | tf_op jit(solution)/shard_map/convert_element_type | solution.py:100
  44.7 3.4 %collective-permute-start.1 = (bf16[1,8,256]{2,1,0:T(8,128)(2,1)S(1)}, bf16[1,8,256]{2,1,0:T(8,128)(2,1)S(1)}, u32[]{:S(2)}, u32[]{:S(2)}) collective-permute-start(bf16[1,8,256]{2,1,0:T(8,128)(2,1)S(1)} %get-tuple-element.13), channel_id=1, source_target_pairs={{0,2},{2,4},{4,6},{1,3},{3,5},{5,7},{8,10},{10,12},{12,14},{9,11},... | collective-permute-start | bytes 12296 | tf_op jit(solution)/shard_map/ppermute | solution.py:19
  48.1 1.3 %collective-permute-start.2 = (bf16[1,8,256]{2,1,0:T(8,128)(2,1)S(1)}, bf16[1,8,256]{2,1,0:T(8,128)(2,1)S(1)}, u32[]{:S(2)}, u32[]{:S(2)}) collective-permute-start(bf16[1,8,256]{2,1,0:T(8,128)(2,1)S(1)} %get-tuple-element.14), channel_id=1, source_target_pairs={{2,0},{4,2},{6,4},{3,1},{5,3},{7,5},{10,8},{12,10},{14,12},{11,9},... | collective-permute-start | bytes 12296 | tf_op jit(solution)/shard_map/ppermute | solution.py:21
  49.4 1.5 %collective-permute-start = (bf16[2,8,256]{2,1,0:T(8,128)(2,1)S(1)}, bf16[2,8,256]{2,1,0:T(8,128)(2,1)S(1)}, u32[]{:S(2)}, u32[]{:S(2)}) collective-permute-start(bf16[2,8,256]{2,1,0:T(8,128)(2,1)S(1)} %pad_maximum_fusion.4), channel_id=1, source_target_pairs={{1,0},{0,1},{3,2},{2,3},{5,4},{4,5},{7,6},{6,7},{9,8},{8,9},{11,10... | collective-permute-start | bytes 24584 | tf_op jit(solution)/shard_map/ppermute | solution.py:31
  50.9 0.8 copy.16
  51.8 1.8 %collective-permute-done.2 = bf16[1,8,256]{2,1,0:T(8,128)(2,1)S(1)} collective-permute-done((bf16[1,8,256]{2,1,0:T(8,128)(2,1)S(1)}, bf16[1,8,256]{2,1,0:T(8,128)(2,1)S(1)}, u32[]{:S(2)}, u32[]{:S(2)}) %collective-permute-start.2) | collective-permute-done | bytes 4128 | tf_op jit(solution)/shard_map/ppermute | solution.py:21
  53.6 1.5 %collective-permute-start.4 = (bf16[26,8,256]{2,1,0:T(8,128)(2,1)S(1)}, bf16[26,8,256]{2,1,0:T(8,128)(2,1)S(1)}, u32[]{:S(2)}, u32[]{:S(2)}) collective-permute-start(bf16[26,8,256]{2,1,0:T(8,128)(2,1)S(1)} %pad_maximum_fusion.2), channel_id=1, source_target_pairs={{1,0},{0,1},{3,2},{2,3},{5,4},{4,5},{7,6},{6,7},{9,8},{8,9},{11,10... | collective-permute-start | bytes 319496 | tf_op jit(solution)/shard_map/ppermute | solution.py:21
  55.2 0.6 collective-permute-start.3
  55.7 1.4 %fusion.3 = f32[3,24,8,3,24]{4,0,2,3,1:T(4,128)S(1)} fusion(s32[24,9,8]{1,2,0:T(8,128)S(1)} %broadcast_add_fusion, f32[24,9,3]{1,2,0:T(4,128)S(1)} %copy.16, f32[24,9,3]{1,2,0:T(4,128)S(1)} %fusion.77), kind=kOutput, calls=%fused_computation.3 | convolution fusion | flops 4522392 | bytes 177984 | tf_op jit(solution)/shard_map/ikb,ikr,ikjq->bijrq/dot_general | solution.py:65
  57.1 0.7 copy.25
  57.8 0.4 reshape.64
  58.4 1.5 %collective-permute-done.3 = bf16[26,8,256]{2,1,0:T(8,128)(2,1)S(1)} collective-permute-done((bf16[26,8,256]{2,1,0:T(8,128)(2,1)S(1)}, bf16[26,8,256]{2,1,0:T(8,128)(2,1)S(1)}, u32[]{:S(2)}, u32[]{:S(2)}) %collective-permute-start.3) | collective-permute-done | bytes 106528 | tf_op jit(solution)/shard_map/ppermute | solution.py:19
  60.0 0.5 fusion.6
  60.5 0.5 copy-done.1
  61.3 0.3 fusion.92
  61.6 0.2 multiply_reduce_fusion.1
  61.9 0.5 fusion.8
  62.4 1.2 %collective-permute-start.5 = (bf16[2,8,256]{2,1,0:T(8,128)(2,1)S(1)}, bf16[2,8,256]{2,1,0:T(8,128)(2,1)S(1)}, u32[]{:S(2)}, u32[]{:S(2)}) collective-permute-start(bf16[2,8,256]{2,1,0:T(8,128)(2,1)S(1)} %pad_maximum_fusion.5), channel_id=1, source_target_pairs={{1,0},{0,1},{3,2},{2,3},{5,4},{4,5},{7,6},{6,7},{9,8},{8,9},{11,10... | collective-permute-start | bytes 24584 | tf_op jit(solution)/shard_map/ppermute | solution.py:31
  63.6 4.1 %collective-permute-start.6 = (bf16[1,8,256]{2,1,0:T(8,128)(2,1)S(1)}, bf16[1,8,256]{2,1,0:T(8,128)(2,1)S(1)}, u32[]{:S(2)}, u32[]{:S(2)}) collective-permute-start(bf16[1,8,256]{2,1,0:T(8,128)(2,1)S(1)} %get-tuple-element.11), channel_id=1, source_target_pairs={{0,2},{2,4},{4,6},{1,3},{3,5},{5,7},{8,10},{10,12},{12,14},{9,11},... | collective-permute-start | bytes 12296 | tf_op jit(solution)/shard_map/ppermute | solution.py:19
  67.7 1.3 %collective-permute-start.7 = (bf16[1,8,256]{2,1,0:T(8,128)(2,1)S(1)}, bf16[1,8,256]{2,1,0:T(8,128)(2,1)S(1)}, u32[]{:S(2)}, u32[]{:S(2)}) collective-permute-start(bf16[1,8,256]{2,1,0:T(8,128)(2,1)S(1)} %get-tuple-element.12), channel_id=1, source_target_pairs={{2,0},{4,2},{6,4},{3,1},{5,3},{7,5},{10,8},{12,10},{14,12},{11,9},... | collective-permute-start | bytes 12296 | tf_op jit(solution)/shard_map/ppermute | solution.py:21
  69.0 4.2 %collective-permute-done.7 = bf16[1,8,256]{2,1,0:T(8,128)(2,1)S(1)} collective-permute-done((bf16[1,8,256]{2,1,0:T(8,128)(2,1)S(1)}, bf16[1,8,256]{2,1,0:T(8,128)(2,1)S(1)}, u32[]{:S(2)}, u32[]{:S(2)}) %collective-permute-start.7) | collective-permute-done | bytes 4128 | tf_op jit(solution)/shard_map/ppermute | solution.py:21
  73.3 1.0 %collective-permute-start.9 = (bf16[26,8,256]{2,1,0:T(8,128)(2,1)S(1)}, bf16[26,8,256]{2,1,0:T(8,128)(2,1)S(1)}, u32[]{:S(2)}, u32[]{:S(2)}) collective-permute-start(bf16[26,8,256]{2,1,0:T(8,128)(2,1)S(1)} %pad_maximum_fusion.3), channel_id=1, source_target_pairs={{1,0},{0,1},{3,2},{2,3},{5,4},{4,5},{7,6},{6,7},{9,8},{8,9},{11,10... | collective-permute-start | bytes 319496 | tf_op jit(solution)/shard_map/ppermute | solution.py:21
  74.2 1.1 %collective-permute-start.8 = (bf16[26,8,256]{2,1,0:T(8,128)(2,1)S(1)}, bf16[26,8,256]{2,1,0:T(8,128)(2,1)S(1)}, u32[]{:S(2)}, u32[]{:S(2)}) collective-permute-start(bf16[26,8,256]{2,1,0:T(8,128)(2,1)S(1)} %pad_maximum_fusion.3), channel_id=1, source_target_pairs={{0,1},{1,0},{2,3},{3,2},{4,5},{5,4},{6,7},{7,6},{8,9},{9,8},{10,11... | collective-permute-start | bytes 319496 | tf_op jit(solution)/shard_map/ppermute | solution.py:19
  75.4 2.7 %collective-permute-done.9 = bf16[26,8,256]{2,1,0:T(8,128)(2,1)S(1)} collective-permute-done((bf16[26,8,256]{2,1,0:T(8,128)(2,1)S(1)}, bf16[26,8,256]{2,1,0:T(8,128)(2,1)S(1)}, u32[]{:S(2)}, u32[]{:S(2)}) %collective-permute-start.9) | collective-permute-done | bytes 106528 | tf_op jit(solution)/shard_map/ppermute | solution.py:21
  78.0 1.1 %collective-permute-done.8 = bf16[26,8,256]{2,1,0:T(8,128)(2,1)S(1)} collective-permute-done((bf16[26,8,256]{2,1,0:T(8,128)(2,1)S(1)}, bf16[26,8,256]{2,1,0:T(8,128)(2,1)S(1)}, u32[]{:S(2)}, u32[]{:S(2)}) %collective-permute-start.8) | collective-permute-done | bytes 106528 | tf_op jit(solution)/shard_map/ppermute | solution.py:19
  79.3 0.5 fusion.7
  80.2 0.3 fusion.93
  80.7 1.1 %fusion.11 = bf16[1,24,8,256]{3,2,1,0:T(8,128)(2,1)} fusion(f32[192,256]{1,0:T(8,128)S(1)} %get-tuple-element.22, bf16[512,256]{1,0:T(8,128)(2,1)S(1)} %copy-done, bf16[256,512]{1,0:T(8,128)(2,1)S(1)} %copy-done.2, f32[512]{0:T(512)S(1)} %copy-done.3, f32[192]{0:T(256)S(1)} %add_rsqrt_fusion, f32[192]{0:T(256)S(1)} %broadcast_multiply_fusion, ...), kind=kOutput, calls=%fused_computation.22 | convolution fusion | flops 101941248 | bytes 823808 | tf_op jit(solution)/shard_map/dot_general | solution.py:85
  (41 shorter events, 1.6 us)
Async XLA Ops:
  6.5 55.3 %copy-start = (bf16[512,256]{1,0:T(8,128)(2,1)S(1)}, bf16[512,256]{1,0:T(8,128)(2,1)}, u32[]{:S(2)}) copy-start(bf16[512,256]{1,0:T(8,128)(2,1)} %param.21) | copy-start | bytes 786436
  6.5 37.2 %all-reduce.2.cloned.1.call-start = ((), (), s32[]{:S(2)}) async-start(), calls=%async_computation | async-start | bytes 196608 | tf_op jit(solution)/shard_map/psum | solution.py:99
  44.7 7.1 %collective-permute-start.1 = (bf16[1,8,256]{2,1,0:T(8,128)(2,1)S(1)}, bf16[1,8,256]{2,1,0:T(8,128)(2,1)S(1)}, u32[]{:S(2)}, u32[]{:S(2)}) collective-permute-start(bf16[1,8,256]{2,1,0:T(8,128)(2,1)S(1)} %get-tuple-element.13), channel_id=1, source_target_pairs={{0,2},{2,4},{4,6},{1,3},{3,5},{5,7},{8,10},{10,12},{12,14},{9,11},... | collective-permute-start | bytes 12296 | tf_op jit(solution)/shard_map/ppermute | solution.py:19
  48.1 5.5 %collective-permute-start.2 = (bf16[1,8,256]{2,1,0:T(8,128)(2,1)S(1)}, bf16[1,8,256]{2,1,0:T(8,128)(2,1)S(1)}, u32[]{:S(2)}, u32[]{:S(2)}) collective-permute-start(bf16[1,8,256]{2,1,0:T(8,128)(2,1)S(1)} %get-tuple-element.14), channel_id=1, source_target_pairs={{2,0},{4,2},{6,4},{3,1},{5,3},{7,5},{10,8},{12,10},{14,12},{11,9},... | collective-permute-start | bytes 12296 | tf_op jit(solution)/shard_map/ppermute | solution.py:21
  49.4 4.2 %collective-permute-start = (bf16[2,8,256]{2,1,0:T(8,128)(2,1)S(1)}, bf16[2,8,256]{2,1,0:T(8,128)(2,1)S(1)}, u32[]{:S(2)}, u32[]{:S(2)}) collective-permute-start(bf16[2,8,256]{2,1,0:T(8,128)(2,1)S(1)} %pad_maximum_fusion.4), channel_id=1, source_target_pairs={{1,0},{0,1},{3,2},{2,3},{5,4},{4,5},{7,6},{6,7},{9,8},{8,9},{11,10... | collective-permute-start | bytes 24584 | tf_op jit(solution)/shard_map/ppermute | solution.py:31
  53.6 4.8 %collective-permute-start.4 = (bf16[26,8,256]{2,1,0:T(8,128)(2,1)S(1)}, bf16[26,8,256]{2,1,0:T(8,128)(2,1)S(1)}, u32[]{:S(2)}, u32[]{:S(2)}) collective-permute-start(bf16[26,8,256]{2,1,0:T(8,128)(2,1)S(1)} %pad_maximum_fusion.2), channel_id=1, source_target_pairs={{1,0},{0,1},{3,2},{2,3},{5,4},{4,5},{7,6},{6,7},{9,8},{8,9},{11,10... | collective-permute-start | bytes 319496 | tf_op jit(solution)/shard_map/ppermute | solution.py:21
  55.2 4.7 %collective-permute-start.3 = (bf16[26,8,256]{2,1,0:T(8,128)(2,1)S(1)}, bf16[26,8,256]{2,1,0:T(8,128)(2,1)S(1)}, u32[]{:S(2)}, u32[]{:S(2)}) collective-permute-start(bf16[26,8,256]{2,1,0:T(8,128)(2,1)S(1)} %pad_maximum_fusion.2), channel_id=1, source_target_pairs={{0,1},{1,0},{2,3},{3,2},{4,5},{5,4},{6,7},{7,6},{8,9},{9,8},{10,11... | collective-permute-start | bytes 319496 | tf_op jit(solution)/shard_map/ppermute | solution.py:19
  60.0 1.0 %copy-start.1 = (bf16[3,256,256]{2,1,0:T(8,128)(2,1)S(1)}, bf16[3,256,256]{2,1,0:T(8,128)(2,1)}, u32[]{:S(2)}) copy-start(bf16[3,256,256]{2,1,0:T(8,128)(2,1)} %param.17) | copy-start | bytes 1179652
  61.0 0.9 %copy-start.2 = (bf16[256,512]{1,0:T(8,128)(2,1)S(1)}, bf16[256,512]{1,0:T(8,128)(2,1)}, u32[]{:S(2)}) copy-start(bf16[256,512]{1,0:T(8,128)(2,1)} %param.19) | copy-start | bytes 786436
  61.0 1.0 %copy-start.3 = (f32[512]{0:T(512)S(1)}, f32[512]{0:T(512)}, u32[]{:S(2)}) copy-start(f32[512]{0:T(512)} %param.20) | copy-start | bytes 6148
  61.0 1.0 %copy-start.4 = (f32[256]{0:T(256)S(1)}, f32[256]{0:T(256)}, u32[]{:S(2)}) copy-start(f32[256]{0:T(256)} %param.18) | copy-start | bytes 3076
  62.4 10.8 %collective-permute-start.5 = (bf16[2,8,256]{2,1,0:T(8,128)(2,1)S(1)}, bf16[2,8,256]{2,1,0:T(8,128)(2,1)S(1)}, u32[]{:S(2)}, u32[]{:S(2)}) collective-permute-start(bf16[2,8,256]{2,1,0:T(8,128)(2,1)S(1)} %pad_maximum_fusion.5), channel_id=1, source_target_pairs={{1,0},{0,1},{3,2},{2,3},{5,4},{4,5},{7,6},{6,7},{9,8},{8,9},{11,10... | collective-permute-start | bytes 24584 | tf_op jit(solution)/shard_map/ppermute | solution.py:31
  63.6 5.4 %collective-permute-start.6 = (bf16[1,8,256]{2,1,0:T(8,128)(2,1)S(1)}, bf16[1,8,256]{2,1,0:T(8,128)(2,1)S(1)}, u32[]{:S(2)}, u32[]{:S(2)}) collective-permute-start(bf16[1,8,256]{2,1,0:T(8,128)(2,1)S(1)} %get-tuple-element.11), channel_id=1, source_target_pairs={{0,2},{2,4},{4,6},{1,3},{3,5},{5,7},{8,10},{10,12},{12,14},{9,11},... | collective-permute-start | bytes 12296 | tf_op jit(solution)/shard_map/ppermute | solution.py:19
  67.7 5.5 %collective-permute-start.7 = (bf16[1,8,256]{2,1,0:T(8,128)(2,1)S(1)}, bf16[1,8,256]{2,1,0:T(8,128)(2,1)S(1)}, u32[]{:S(2)}, u32[]{:S(2)}) collective-permute-start(bf16[1,8,256]{2,1,0:T(8,128)(2,1)S(1)} %get-tuple-element.12), channel_id=1, source_target_pairs={{2,0},{4,2},{6,4},{3,1},{5,3},{7,5},{10,8},{12,10},{14,12},{11,9},... | collective-permute-start | bytes 12296 | tf_op jit(solution)/shard_map/ppermute | solution.py:21
  73.3 4.8 %collective-permute-start.9 = (bf16[26,8,256]{2,1,0:T(8,128)(2,1)S(1)}, bf16[26,8,256]{2,1,0:T(8,128)(2,1)S(1)}, u32[]{:S(2)}, u32[]{:S(2)}) collective-permute-start(bf16[26,8,256]{2,1,0:T(8,128)(2,1)S(1)} %pad_maximum_fusion.3), channel_id=1, source_target_pairs={{1,0},{0,1},{3,2},{2,3},{5,4},{4,5},{7,6},{6,7},{9,8},{8,9},{11,10... | collective-permute-start | bytes 319496 | tf_op jit(solution)/shard_map/ppermute | solution.py:21
  74.2 5.0 %collective-permute-start.8 = (bf16[26,8,256]{2,1,0:T(8,128)(2,1)S(1)}, bf16[26,8,256]{2,1,0:T(8,128)(2,1)S(1)}, u32[]{:S(2)}, u32[]{:S(2)}) collective-permute-start(bf16[26,8,256]{2,1,0:T(8,128)(2,1)S(1)} %pad_maximum_fusion.3), channel_id=1, source_target_pairs={{0,1},{1,0},{2,3},{3,2},{4,5},{5,4},{6,7},{7,6},{8,9},{9,8},{10,11... | collective-permute-start | bytes 319496 | tf_op jit(solution)/shard_map/ppermute | solution.py:19
Sparse Core Ops, SparseCore 0:
  9.7 33.9 all-reduce.1
where the time goes:
time: 89 us; the launch traced here: 88.6 us
  waiting for transfers between devices  45.3 us (51%)
  starting transfers between devices  17 us (19%)
  between operations  13.6 us (15%)
  matrix products  6.94 us (8%)
  local copies, waits for them, and re-layouts  3.47 us (4%)
  other arithmetic  2.27 us (3%)
    psum x1, waiting for transfers between devices, shards(): lax.psum(partial_base.astype(jnp.bfloat16), 'member').astype(jnp.float32)  33.8 us
    ppermute x4, starting transfers between devices, padded(): lax.ppermute(tail, axis, [(i, (i + 1) % count) for i in range(ends)])  9.21 us
    ppermute x4, waiting for transfers between devices, padded(): lax.ppermute(head, axis, [((i + 1) % count, i) for i in range(ends)])  8.82 us
    ppermute x4, starting transfers between devices, padded(): lax.ppermute(head, axis, [((i + 1) % count, i) for i in range(ends)])  5.07 us
    ppermute x2, starting transfers between devices, passed_along(): return lax.ppermute(block, axis, route)  2.74 us
    ppermute x4, waiting for transfers between devices, padded(): lax.ppermute(tail, axis, [(i, (i + 1) % count) for i in range(ends)])  2.63 us
    unnamed x12, local copies, waits for them, and re-layouts  2.16 us
  transfers between devices with their start and end apart: 11, of which 7 were waited for; matrix products, arithmetic and copies ran while one was open for 6% of the time, Pallas kernels for 0%

commit v1 on v0

--- a/solution.py
+++ b/solution.py
@@ -1,14 +1,20 @@
+import functools
+
 import jax
 import jax.numpy as jnp
 from jax import lax
+from jax.experimental import pallas as pl
+from jax.experimental.pallas import tpu as pltpu
 from jax.sharding import PartitionSpec as P
 
 B = 3
 HW = 8
 PASSES = 2
-
-
-def padded(cells, sides, width, closed):
+K = 9
+GROUP = 6
+
+
+def ring_padded(cells, sides, width, closed):
     for axis, dim in sides:
         count = lax.axis_size(axis)
         ends = count if closed else count - 1
@@ -25,30 +31,20 @@
     return cells
 
 
-def passed_along(block, axis, distance):
-    devices = range(lax.axis_size(axis))
-    route = [((i - distance) % len(devices), i) for i in devices]
-    return lax.ppermute(block, axis, route)
-
-
-def fix_poles(rows, flipped):
+def extend(state):
+    count = lax.axis_size("lon")
+    rows = ring_padded(state, (("lat", 0),), 1, False)
+    edges = jnp.stack([state[0], state[-1]])
+    flipped = lax.ppermute(edges, "lon", [(i, (i + count // 2) % count) for i in range(count)])
     band = lax.axis_index("lat")
     last_band = lax.axis_size("lat") - 1
     top = jnp.where(band == 0, flipped[0], rows[0])
     bottom = jnp.where(band == last_band, flipped[1], rows[-1])
-    return jnp.concatenate([top[None], rows[1:-1], bottom[None]], axis=0)
-
-
-def extend(state):
-    half = lax.axis_size("lon") // 2
-    rows = padded(state, (("lat", 0),), 1, False)
-    edges = jnp.stack([state[0], state[-1]])
-    flipped = passed_along(edges, "lon", half)
-    rows = fix_poles(rows, flipped)
-    return padded(rows, (("lon", 1),), HW, True)
-
-
-def one_pass(state, lat_offsets, lon_offsets, psi, w_disco, norm_gain, w_up, bias_up, w_down):
+    rows = jnp.concatenate([top[None], rows[1:-1], bottom[None]], axis=0)
+    return ring_padded(rows, (("lon", 1),), HW, True)
+
+
+def window_pass(state, lat_offsets, lon_offsets, psi, w_disco, norm_gain, w_up, bias_up, w_down):
     row_count, col_count, width = state.shape
     extended = extend(state)
     span = col_count + 2 * HW
@@ -86,7 +82,7 @@
     return result.astype(jnp.bfloat16).reshape(row_count, col_count, width)
 
 
-def shards(
+def window_shards(
     analysis, noise, w_in, lat_offsets, lon_offsets, psi, w_disco, norm_gain, w_up, bias_up, w_down
 ):
     row_count, col_count, quarter = analysis.shape
@@ -100,15 +96,366 @@
     state = (base + noise[0].reshape(-1, width).astype(jnp.float32)).astype(jnp.bfloat16)
     state = state.reshape(row_count, col_count, width)
     for step in range(PASSES):
-        state = one_pass(
+        state = window_pass(
             state, lat_offsets, lon_offsets, psi, w_disco, norm_gain, w_up, bias_up, w_down
         )
     return state[None]
 
 
+def border_kernel(border_ref):
+    border_ref[...] = jnp.zeros_like(border_ref)
+
+
+def weights_kernel(
+    lat_ref, lon_ref, psi_ref, w_in_ref, w_disco_ref, w_up_ref, w_down_ref, gain_ref, bias_ref,
+    weights_ref, spread_ref, disco_out, up_out, down_out, gain_out, bias_out, in_ref, sems,
+):
+    pairs = (
+        (w_in_ref, in_ref), (w_disco_ref, disco_out), (w_up_ref, up_out),
+        (w_down_ref, down_out), (gain_ref, gain_out), (bias_ref, bias_out),
+    )
+    copies = [
+        pltpu.make_async_copy(source, target, sems.at[i]) for i, (source, target) in enumerate(pairs)
+    ]
+    for copy in copies:
+        copy.start()
+    f32 = jnp.float32
+    rows = lat_ref.shape[1]
+    band = lax.axis_index("lat")
+    row = lax.broadcasted_iota(jnp.int32, (K, rows), 1)
+    up, along = lat_ref[...], lon_ref[...]
+    crossing = ((band == 0) & (row == 0) & (up < 0)) | (
+        (band == lax.axis_size("lat") - 1) & (row == rows - 1) & (up > 0)
+    )
+    place = jnp.where(crossing, 1, up + 1) * 16 + ((along + jnp.where(crossing, 8, 0)) & 15)
+    spot = lax.broadcasted_iota(jnp.int32, (48, rows), 0)
+    sums = [jnp.zeros((48, rows), f32) for _ in range(B)]
+    for k in range(K):
+        hit = spot == place[k : k + 1]
+        for b in range(B):
+            sums[b] = sums[b] + jnp.where(hit, psi_ref[k, b : b + 1, :], 0.0)
+    lines = [
+        jnp.transpose(jnp.pad(part, ((0, 80), (0, 128 - rows))))[:rows] for part in sums
+    ]
+    col = lax.broadcasted_iota(jnp.int32, (16, 128), 0)
+    straight = lax.broadcasted_iota(jnp.int32, (16, 128), 1) % 16 >= col
+    for i in range(rows):
+        shift = (i + 1) % GROUP * 16
+        for b in range(B):
+            line = jnp.broadcast_to(lines[b][i : i + 1], (16, 128))
+            turned = jnp.where(
+                straight,
+                pltpu.roll(line, shift, 1, stride=1, stride_axis=0),
+                pltpu.roll(line, (shift + 112) % 128, 1, stride=1, stride_axis=0),
+            )
+            weights_ref[pl.ds((i * B + b) * 16, 16), :] = turned.astype(jnp.bfloat16)
+    member = lax.axis_index("member")
+    quarter = w_in_ref.shape[0] // 4
+    copies[0].wait()
+    even = member - member % 2
+    groups = (
+        member, member ^ 1, member ^ 2, member ^ 3, even, even ^ 1, even ^ 3, even ^ 2
+    )
+    for place, group in enumerate(groups):
+        spread_ref[pl.ds(place * quarter, quarter), :] = in_ref[
+            pl.ds(pl.multiple_of(group * quarter, quarter), quarter), :
+        ]
+    for copy in copies[1:]:
+        copy.wait()
+
+
+def start_kernel(
+    chip_ref, x_ref, sent_ref, got_ref, noise_ref, from_y_ref, spread_ref, weights_ref, border_ref,
+    state_ref, first_ref, second_ref,
+):
+    f32, bf16 = jnp.float32, jnp.bfloat16
+    rows, cols, width = noise_ref.shape
+    wide = lambda block: block.astype(f32).reshape(rows * cols, block.shape[2])
+    sent, got = wide(sent_ref[...]), wide(got_ref[...])
+    even_core = lax.axis_index("member") % 2 == 0
+    along_y, diagonal = jnp.where(even_core, sent, got), jnp.where(even_core, got, sent)
+
+    def base_of(parts, first):
+        analysis = jnp.concatenate(parts, axis=1).astype(bf16)
+        base = jnp.dot(
+            analysis, spread_ref[pl.ds(first, analysis.shape[1]), :], preferred_element_type=f32
+        )
+        return base.reshape(rows, cols, width)
+
+    own = base_of([wide(chip_ref[pl.ds(0, rows)]), wide(x_ref[pl.ds(0, rows)])], 0)
+    other = base_of([along_y, diagonal], width)
+    state = jnp.concatenate(
+        [own + noise_ref[...].astype(f32), other + from_y_ref[...].astype(f32)], axis=1
+    )
+    state = state.astype(bf16).reshape(rows * 16, width)
+    state_ref[pl.ds(0, 32), :] = border_ref[...]
+    state_ref[pl.ds(32, rows * 16), :] = state
+    state_ref[pl.ds(32 + rows * 16, 32), :] = border_ref[...]
+    even = lax.axis_index("lat") % 2 == 0
+    for ref, last in ((first_ref, even), (second_ref, jnp.logical_not(even))):
+        line = pl.multiple_of(jnp.where(last, (rows - 1) * B * 16, 0), 16)
+        cell = pl.multiple_of(jnp.where(last, rows * 16, 32), 16)
+        ref[pl.ds(0, 32), :] = state_ref[pl.ds(cell, 32), pl.ds(0, 128)]
+        ref[pl.ds(32, 32), :] = state_ref[pl.ds(cell, 32), pl.ds(128, 128)]
+        ref[pl.ds(64, B * 16), :] = weights_ref[pl.ds(line, B * 16), :]
+
+
+def mixed(weights, state, count, width):
+    mix = jnp.dot(weights, state, preferred_element_type=jnp.float32)
+    return mix.reshape(count, B, 16, width)
+
+
+def cell_block(before, mix, w_disco_ref, gain_ref, w_up_ref, bias_ref, w_down_ref):
+    f32, bf16 = jnp.float32, jnp.bfloat16
+    width = before.shape[1]
+    inner = before + jnp.dot(
+        mix, w_disco_ref[...].reshape(B * width, width), preferred_element_type=f32
+    )
+    mean = jnp.mean(inner, axis=1, keepdims=True)
+    variance = jnp.mean(inner * inner, axis=1, keepdims=True) - mean * mean
+    scale = lax.rsqrt(jnp.maximum(variance, 0.0) + 1e-05)
+    normed = ((inner - mean) * scale * gain_ref[...]).astype(bf16)
+    hidden = jax.nn.gelu(
+        jnp.dot(normed, w_up_ref[...], preferred_element_type=f32) + bias_ref[...]
+    ).astype(bf16)
+    return inner + jnp.dot(hidden, w_down_ref[...], preferred_element_type=f32)
+
+
+def mixed_rows(low, high, rows, weights_ref, state_ref):
+    first = low - low % GROUP
+    reach = min(GROUP + 2, rows + 4 - first) * 16
+    return mixed(
+        weights_ref[pl.ds((low - 1) * B * 16, (high - low) * B * 16), pl.ds(0, reach)],
+        state_ref[pl.ds(first * 16, reach), :],
+        high - low,
+        state_ref.shape[1],
+    )
+
+
+def inner_kernel(
+    state_ref, weights_ref, w_disco_ref, gain_ref, w_up_ref, bias_ref, w_down_ref,
+    near_ref, out_ref, next_ref, mix_ref, own_mix_ref,
+):
+    f32, bf16 = jnp.float32, jnp.bfloat16
+    width = state_ref.shape[1]
+    rows, cols = out_ref.shape[0] + 4, out_ref.shape[1]
+    block = functools.partial(
+        cell_block, w_disco_ref=w_disco_ref, gain_ref=gain_ref, w_up_ref=w_up_ref,
+        bias_ref=bias_ref, w_down_ref=w_down_ref,
+    )
+    for first in range(0, rows, GROUP):
+        low, high = max(first, 2), min(first + GROUP, rows)
+        mix = mixed_rows(low, high, rows, weights_ref, state_ref)
+        for i in range(low, high):
+            for b in range(B):
+                mix_ref[pl.ds((i - 2) * 16, 16), pl.ds(b * width, width)] = mix[i - low, b].astype(bf16)
+    after = block(
+        state_ref[pl.ds(48, (rows - 2) * 16), :].astype(f32), mix_ref[...]
+    ).astype(bf16)
+    border = jnp.zeros((48, width), bf16)
+    next_ref[pl.ds(0, 48), :] = border
+    next_ref[pl.ds(48, (rows - 2) * 16), :] = after
+    next_ref[pl.ds(16 + rows * 16, 48), :] = border
+    near_ref[pl.ds(0, 32), :] = after[:32]
+    near_ref[pl.ds(32, 32), :] = after[(rows - 4) * 16 :]
+    for first in range(0, rows - 1, GROUP):
+        low, high = max(first, 3), min(first + GROUP, rows - 1)
+        mix = mixed_rows(low, high, rows, weights_ref, next_ref)
+        for i in range(low, high):
+            for b in range(B):
+                own_mix_ref[pl.ds((i - 3) * cols, cols), pl.ds(b * width, width)] = mix[i - low, b, :cols]
+    own = next_ref[pl.ds(64, (rows - 4) * 16), :].astype(f32).reshape(rows - 4, 16, width)[:, :cols]
+    result = block(own.reshape((rows - 4) * cols, width), own_mix_ref[...].astype(bf16))
+    out_ref[...] = result.reshape(rows - 4, cols, width).astype(bf16)
+
+
+def edge_kernel(
+    state_ref, near_ref, inner_ref, first_ref, second_ref, weights_ref,
+    w_disco_ref, gain_ref, w_up_ref, bias_ref, w_down_ref, out_ref, next_ref, halo_ref, last_ref, sems,
+):
+    f32, bf16 = jnp.float32, jnp.bfloat16
+    rows, cols, width = out_ref.shape
+    block = functools.partial(
+        cell_block, w_disco_ref=w_disco_ref, gain_ref=gain_ref, w_up_ref=w_up_ref,
+        bias_ref=bias_ref, w_down_ref=w_down_ref,
+    )
+    inner_copy = pltpu.make_async_copy(inner_ref, out_ref.at[pl.ds(2, rows - 4)], sems.at[0])
+    inner_copy.start()
+    line = B * 16
+    even = lax.axis_index("lat") % 2 == 0
+    halo_ref[jnp.where(even, 1, 0)] = first_ref[...]
+    halo_ref[jnp.where(even, 0, 1)] = second_ref[...]
+
+    def received(side):
+        return jnp.concatenate([halo_ref[side, :32, :], halo_ref[side, 32:64, :]], axis=1)
+
+    def one_row(mix):
+        return jnp.concatenate([mix[b] for b in range(B)], axis=1)
+
+    top_state = jnp.concatenate([received(0), state_ref[pl.ds(32, 32), :]], axis=0)
+    top_mix = mixed(
+        jnp.concatenate([halo_ref[0, 64:, :], weights_ref[pl.ds(0, line), :]], axis=0)[:, :64],
+        top_state, 2, width,
+    )
+    bottom_state = jnp.concatenate(
+        [state_ref[pl.ds(rows * 16, 32), :], received(1)], axis=0
+    )
+    bottom_mix = mixed(
+        jnp.concatenate(
+            [weights_ref[pl.ds((rows - 1) * line, line), :], halo_ref[1, 64:, :]], axis=0
+        )[:, :64],
+        bottom_state, 2, width,
+    )
+    edge_mix = jnp.concatenate(
+        [one_row(mix[i]) for mix in (top_mix, bottom_mix) for i in range(2)], axis=0
+    ).astype(bf16)
+    edge_state = jnp.concatenate([top_state[16:48], bottom_state[16:48]], axis=0)
+    edge = block(edge_state.astype(f32), edge_mix).astype(bf16)
+    next_ref[...] = jnp.zeros_like(next_ref)
+    next_ref[pl.ds(16, 32), :] = edge[:32]
+    next_ref[pl.ds(48, 32), :] = near_ref[pl.ds(0, 32), :]
+    next_ref[pl.ds((rows - 1) * 16, 32), :] = near_ref[pl.ds(32, 32), :]
+    next_ref[pl.ds((rows + 1) * 16, 32), :] = edge[32:]
+    mixes, own = [], []
+    for low, high in ((1, 3), (rows - 1, rows), (rows, rows + 1)):
+        mix = mixed_rows(low, high, rows, weights_ref, next_ref)
+        for i in range(low, high):
+            mixes.append(one_row(mix[i - low, :, :cols]))
+            own.append(next_ref[pl.ds((i + 1) * 16, 16), :].astype(f32)[:cols])
+    result = block(jnp.concatenate(own, axis=0), jnp.concatenate(mixes, axis=0).astype(bf16))
+    last_ref[...] = result.reshape(4, cols, width).astype(bf16)
+    top_copy = pltpu.make_async_copy(
+        last_ref.at[pl.ds(0, 2)], out_ref.at[pl.ds(0, 2)], sems.at[1]
+    )
+    bottom_copy = pltpu.make_async_copy(
+        last_ref.at[pl.ds(2, 2)], out_ref.at[pl.ds(rows - 2, 2)], sems.at[2]
+    )
+    top_copy.start()
+    bottom_copy.start()
+    inner_copy.wait()
+    top_copy.wait()
+    bottom_copy.wait()
+
+
+def circle_shards(
+    analysis, noise, w_in, lat_offsets, lon_offsets, psi, w_disco, norm_gain, w_up, bias_up, w_down
+):
+    f32, bf16 = jnp.float32, jnp.bfloat16
+    rows, cols, quarter = analysis.shape
+    width = w_in.shape[1]
+    noise = noise[0]
+    bands = lax.axis_size("lat")
+    members = lax.axis_size("member")
+    line = B * 16
+    vmem = pl.BlockSpec(memory_space=pltpu.VMEM)
+    hbm = pl.BlockSpec(memory_space=pltpu.HBM)
+    params = pltpu.CompilerParams(vmem_limit_bytes=12 * 1024 * 1024)
+
+    def shape(*dims, dtype=bf16):
+        return jax.ShapeDtypeStruct(dims, dtype)
+
+    def swapped(block, partner):
+        pairs = [(i, partner(i)) for i in range(2 * members)]
+        return lax.ppermute(block, ("member", "lon"), pairs)
+
+    from_y = swapped(noise, lambda i: i ^ 1)
+    from_core = swapped(analysis, lambda i: i ^ 2)
+    border = pl.pallas_call(
+        border_kernel,
+        out_shape=shape(32, width),
+        out_specs=vmem,
+        cost_estimate=pl.CostEstimate(flops=1_000_000_000, bytes_accessed=16_384, transcendentals=0),
+        compiler_params=params,
+    )()
+    analysis, border = lax.optimization_barrier((analysis, border))
+    chip = jnp.pad(jnp.concatenate([analysis, from_core], axis=2), ((0, 1), (0, 0), (0, 0)))
+    across = swapped(chip, lambda i: i ^ 5 if i & 2 else i ^ 1)
+    from_x = swapped(chip, lambda i: i ^ 4)
+    weights, spread, *dense = pl.pallas_call(
+        weights_kernel,
+        out_shape=(
+            shape(rows * line, 128), shape(8 * quarter, width), shape(*w_disco.shape),
+            shape(*w_up.shape), shape(*w_down.shape), shape(1, width, dtype=f32),
+            shape(1, w_up.shape[1], dtype=f32),
+        ),
+        in_specs=[vmem] * 3 + [hbm] * 6,
+        out_specs=(vmem,) * 7,
+        scratch_shapes=[pltpu.VMEM(w_in.shape, bf16), pltpu.SemaphoreType.DMA((6,))],
+        cost_estimate=pl.CostEstimate(flops=4_000, bytes_accessed=3_000, transcendentals=0),
+        compiler_params=params,
+    )(
+        lat_offsets.T,
+        lon_offsets.T,
+        jnp.transpose(psi, (1, 2, 0)),
+        *(
+            pltpu.with_memory_space_constraint(w, pltpu.HBM)
+            for w in (
+                w_in, w_disco, w_up, w_down, norm_gain.reshape(1, -1), bias_up.reshape(1, -1)
+            )
+        ),
+    )
+    w_disco, w_up, w_down, norm_gain, bias_up = dense
+    dense = (w_disco, norm_gain, w_up, bias_up, w_down)
+
+    across, from_y, weights = lax.optimization_barrier((across, from_y, weights))
+    across = across[:rows]
+    got = swapped(across, lambda i: i ^ 2)
+    state, first, second = pl.pallas_call(
+        start_kernel,
+        out_shape=(shape((rows + 4) * 16, width), shape(64 + line, 128), shape(64 + line, 128)),
+        in_specs=[vmem] * 9,
+        out_specs=(vmem,) * 3,
+        cost_estimate=pl.CostEstimate(flops=200_000_000, bytes_accessed=1_000_000, transcendentals=0),
+        compiler_params=params,
+    )(chip, from_x, across, got, noise, from_y, spread, weights, border)
+    def paired(edge, start):
+        pairs = []
+        for i in range(members):
+            for j in range(bands):
+                k = j + 1 if (j - start) % 2 == 0 else j - 1
+                there = (i, k) if min(j, k) >= start and k < bands else (i ^ 1, j)
+                pairs.append((i * bands + j, there[0] * bands + there[1]))
+        return lax.ppermute(edge, ("member", "lat"), pairs)
+
+    first, second = paired(first, 0), paired(second, 1)
+    near, inner = pl.pallas_call(
+        inner_kernel,
+        out_shape=(shape(64, width), shape(rows - 4, cols, width)),
+        in_specs=[vmem] * 7,
+        out_specs=(vmem, vmem),
+        scratch_shapes=[
+            pltpu.VMEM(((rows + 4) * 16, width), bf16),
+            pltpu.VMEM(((rows - 2) * 16, B * width), bf16),
+            pltpu.VMEM(((rows - 4) * cols, B * width), f32),
+        ],
+        cost_estimate=pl.CostEstimate(
+            flops=800_000_000, bytes_accessed=2_000_000, transcendentals=400_000
+        ),
+        compiler_params=params,
+    )(state, weights, *dense)
+    result = pl.pallas_call(
+        edge_kernel,
+        out_shape=shape(rows, cols, width),
+        in_specs=[vmem] * 11,
+        out_specs=pl.BlockSpec(memory_space=pl.ANY),
+        scratch_shapes=[
+            pltpu.VMEM(((rows + 4) * 16, width), bf16),
+            pltpu.VMEM((2, 64 + line, 128), bf16),
+            pltpu.VMEM((4, cols, width), bf16),
+            pltpu.SemaphoreType.DMA((3,)),
+        ],
+        cost_estimate=pl.CostEstimate(
+            flops=100_000_000, bytes_accessed=2_000_000, transcendentals=50_000
+        ),
+        compiler_params=params,
+    )(state, near, inner, first, second, weights, *dense)
+    return result[None]
+
+
 def solution(mesh):
+    circle = mesh.shape["lon"] == 2 and mesh.shape["member"] == 4
     return jax.shard_map(
-        shards,
+        circle_shards if circle else window_shards,
         mesh=mesh,
         in_specs=(
             P("lat", "lon", "member"),

time: 89 us -> 15.8 us (0.18)
  the two profiles are of different devices: /device:TPU:0 before, /device:TPU:20 now
where the time goes in v1:
time: 15.8 us; the launch traced here: 15.6 us
  Pallas kernels  5.89 us (37%)
  waiting for transfers between devices  5.04 us (32%)
  starting transfers between devices  4.52 us (29%)
    ppermute x5, waiting for transfers between devices, swapped(): return lax.ppermute(block, ('member', 'lon'), pairs)  3.21 us
    ppermute x5, starting transfers between devices, swapped(): return lax.ppermute(block, ('member', 'lon'), pairs)  2.87 us
    pallas_call x1, Pallas kernels, circle_shards(): pl.pallas_call(edge_kernel, out_shape=shape(rows, cols, width), in_specs=...  2.06 us
    pallas_call x1, Pallas kernels, circle_shards(): pl.pallas_call(inner_kernel, out_shape=(shape(64, width), shape(rows - 4,...  2.03 us
    ppermute x2, waiting for transfers between devices, paired(): return lax.ppermute(edge, ('member', 'lat'), pairs)  1.83 us
    ppermute x2, starting transfers between devices, paired(): return lax.ppermute(edge, ('member', 'lat'), pairs)  1.64 us
    pallas_call x1, Pallas kernels, circle_shards(): pl.pallas_call(weights_kernel, out_shape=(shape(rows * line, 128), shape(...  1.58 us
  transfers between devices with their start and end apart: 7, of which 6 were waited for; matrix products, arithmetic and copies ran while one was open for 1% of the time, Pallas kernels for 23%

profile of v1, /device:TPU:20, one launch (start us, length us, event | category | flops | bytes accessed | tf_op | source)
XLA Modules:
  0.0 15.6 jit_solution(15439451650218117603)
XLA Ops:
  0.0 0.0 collective-permute-start
  0.0 0.0 copy-start.4
  0.0 0.6 %collective-permute-start.3 = (bf16[24,8,256]{2,1,0:T(8,128)(2,1)}, bf16[24,8,256]{2,1,0:T(8,128)(2,1)S(1)}, u32[]{:S(2)}, u32[]{:S(2)}) collective-permute-start(bf16[24,8,256]{2,1,0:T(8,128)(2,1)} %bitcast.7), channel_id=1, source_target_pairs={{0,1},{1,0},{8,9},{9,8},{16,17},{17,16},{24,25},{25,24},{2,3},{3,2... | collective-permute-start | bytes 294920 | tf_op jit(solution)/shard_map/ppermute | solution.py:359
  0.6 0.9 %collective-permute-done = bf16[24,8,64]{2,1,0:T(8,128)(2,1)S(1)} collective-permute-done((bf16[24,8,64]{2,1,0:T(8,128)(2,1)}, bf16[24,8,64]{2,1,0:T(8,128)(2,1)S(1)}, u32[]{:S(2)}, u32[]{:S(2)}) %collective-permute-start) | collective-permute-done | bytes 24608 | tf_op jit(solution)/shard_map/ppermute | solution.py:359
  1.4 0.0 copy-done.4
  1.4 0.0 copy-start.1
  1.4 0.0 copy-start.3
  1.4 0.1 fusion.2.chip_ref
  1.5 0.0 copy-start.2
  1.6 0.7 %collective-permute-start.2 = (bf16[25,8,128]{2,1,0:T(8,128)(2,1)S(1)}, bf16[25,8,128]{2,1,0:T(8,128)(2,1)S(1)}, u32[]{:S(2)}, u32[]{:S(2)}) collective-permute-start(bf16[25,8,128]{2,1,0:T(8,128)(2,1)S(1)} %fusion.2.chip_ref), channel_id=1, source_target_pairs={{0,1},{1,0},{8,25},{9,24},{16,17},{17,16},{24,9},{25,8},{2,3},{3,2... | collective-permute-start | bytes 153608 | tf_op jit(solution)/shard_map/ppermute | solution.py:359
  2.3 1.5 %collective-permute-start.1 = (bf16[25,8,128]{2,1,0:T(8,128)(2,1)S(1)}, bf16[25,8,128]{2,1,0:T(8,128)(2,1)S(1)}, u32[]{:S(2)}, u32[]{:S(2)}) collective-permute-start(bf16[25,8,128]{2,1,0:T(8,128)(2,1)S(1)} %fusion.2.chip_ref), channel_id=1, source_target_pairs={{0,16},{1,17},{8,24},{9,25},{16,0},{17,1},{24,8},{25,9},{2,18},{3,... | collective-permute-start | bytes 153608 | tf_op jit(solution)/shard_map/ppermute | solution.py:359
  3.8 0.0 copy-done.1
  3.8 0.0 copy-done.3
  3.8 0.0 copy-done.2
  3.8 1.6 %shard_map.110 = (bf16[1152,128]{1,0:T(8,128)(2,1)S(1)}, bf16[512,256]{1,0:T(8,128)(2,1)S(1)}, bf16[3,256,256]{2,1,0:T(8,128)(2,1)S(1)}, bf16[256,512]{1,0:T(8,1...) custom-call(s32[9,24]{1,0:T(8,128)S(1)} %bitcast.10, ...), custom_call_target="tpu_custom_call" | custom-call | flops 4000 | bytes 3000 | tf_op jit(solution)/shard_map/pallas_call | solution.py:374
  5.4 0.0 copy-start
  5.4 1.1 %collective-permute-done.2 = bf16[25,8,128]{2,1,0:T(8,128)(2,1)S(1)} collective-permute-done((bf16[25,8,128]{2,1,0:T(8,128)(2,1)S(1)}, bf16[25,8,128]{2,1,0:T(8,128)(2,1)S(1)}, u32[]{:S(2)}, u32[]{:S(2)}) %collective-permute-start.2) | collective-permute-done | bytes 51232 | tf_op jit(solution)/shard_map/ppermute | solution.py:359
  6.5 0.0 collective-permute-done.3.from_y_ref
  6.5 0.1 collective-permute-start.4
  6.6 0.2 %collective-permute-done.1.x_ref = bf16[25,8,128]{2,1,0:T(8,128)(2,1)S(1)} collective-permute-done((bf16[25,8,128]{2,1,0:T(8,128)(2,1)S(1)}, bf16[25,8,128]{2,1,0:T(8,128)(2,1)S(1)}, u32[]{:S(2)}, u32[]{:S(2)}) %collective-permute-start.1) | collective-permute-done | bytes 51232 | tf_op jit(solution)/shard_map/ppermute | solution.py:359
  6.8 1.0 %collective-permute-done.4.got_ref = bf16[24,8,128]{2,1,0:T(8,128)(2,1)S(1)} collective-permute-done((bf16[24,8,128]{2,1,0:T(8,128)(2,1)S(1)}, bf16[24,8,128]{2,1,0:T(8,128)(2,1)S(1)}, u32[]{:S(2)}, u32[]{:S(2)}) %collective-permute-start.4) | collective-permute-done | bytes 49184 | tf_op jit(solution)/shard_map/ppermute | solution.py:359
  7.8 0.0 copy-done
  7.8 0.2 %shard_map.111 = (bf16[448,256]{1,0:T(8,128)(2,1)S(1)}, bf16[112,128]{1,0:T(8,128)(2,1)S(1)}, bf16[112,128]{1,0:T(8,128)(2,1)S(1)}) custom-call(bf16[25,8,128]{2,1,0:T(8,128)(2,1)S(1)} %fusion.2.chip_ref, bf16[25,8,128]{2,1,0:T(8,128)(2,1)S(1)} %collective-permute-done.1.x_ref, bf16[24,8,128]{2,1,0:T(8,128)(2,1)S(1)} %slice.3.sent_ref, ...), custom_call_target="tpu_custom_call" | custom-call | flops 200000000 | bytes 1000000 | tf_op jit(solution)/shard_map/pallas_call | solution.py:403
  8.1 1.6 %collective-permute-start.5 = (bf16[112,128]{1,0:T(8,128)(2,1)S(1)}, bf16[112,128]{1,0:T(8,128)(2,1)S(1)}, u32[]{:S(2)}, u32[]{:S(2)}) collective-permute-start(bf16[112,128]{1,0:T(8,128)(2,1)S(1)} %get-tuple-element.37), channel_id=1, source_target_pairs={{0,2},{2,0},{4,6},{6,4},{8,10},{10,8},{12,14},{14,12},{16,18},{18,... | collective-permute-start | bytes 86024 | tf_op jit(solution)/shard_map/ppermute | solution.py:418
  9.7 0.0 collective-permute-start.6
  9.7 2.0 %shard_map.112 = (bf16[64,256]{1,0:T(8,128)(2,1)S(1)}, bf16[20,8,256]{2,1,0:T(8,128)(2,1)S(1)}) custom-call(bf16[448,256]{1,0:T(8,128)(2,1)S(1)} %get-tuple-element.29.state_ref, bf16[1152,128]{1,0:T(8,128)(2,1)S(1)} %get-tuple-element.27.weights_ref, bf16[3,256,256]{2,1,0:T(8,128)(2,1)S(1)} %get-tuple-element.30.w_disco_ref, ...), custom_call_target="tpu_custom_call" | custom-call | flops 800000000 | bytes 2000000 | tf_op jit(solution)/shard_map/pallas_call | solution.py:421
  11.7 0.3 %collective-permute-done.5.first_ref = bf16[112,128]{1,0:T(8,128)(2,1)S(1)} collective-permute-done((bf16[112,128]{1,0:T(8,128)(2,1)S(1)}, bf16[112,128]{1,0:T(8,128)(2,1)S(1)}, u32[]{:S(2)}, u32[]{:S(2)}) %collective-permute-start.5) | collective-permute-done | bytes 28704 | tf_op jit(solution)/shard_map/ppermute | solution.py:418
  12.0 1.6 %collective-permute-done.6.second_ref = bf16[112,128]{1,0:T(8,128)(2,1)S(1)} collective-permute-done((bf16[112,128]{1,0:T(8,128)(2,1)S(1)}, bf16[112,128]{1,0:T(8,128)(2,1)S(1)}, u32[]{:S(2)}, u32[]{:S(2)}) %collective-permute-start.6) | collective-permute-done | bytes 28704 | tf_op jit(solution)/shard_map/ppermute | solution.py:418
  13.6 2.1 %shard_map.113 = bf16[24,8,256]{2,1,0:T(8,128)(2,1)} custom-call(bf16[448,256]{1,0:T(8,128)(2,1)S(1)} %get-tuple-element.29.state_ref, bf16[64,256]{1,0:T(8,128)(2,1)S(1)} %get-tuple-element.35.near_ref, bf16[20,8,256]{2,1,0:T(8,128)(2,1)S(1)} %get-tuple-element.36.inner_ref, bf16[112,128]{1,0:T(8,128)(2,1)S(1)} %collective-permute-done.5.first_ref, ...), custom_call_target="tpu_custom_call" | custom-call | flops 100000000 | bytes 2000000 | tf_op jit(solution)/shard_map/pallas_call | solution.py:436
  (2 shorter events, 0.0 us)
Async XLA Ops:
  0.0 1.4 %collective-permute-start = (bf16[24,8,64]{2,1,0:T(8,128)(2,1)}, bf16[24,8,64]{2,1,0:T(8,128)(2,1)S(1)}, u32[]{:S(2)}, u32[]{:S(2)}) collective-permute-start(bf16[24,8,64]{2,1,0:T(8,128)(2,1)} %param.11), channel_id=1, source_target_pairs={{0,8},{1,9},{8,0},{9,1},{16,24},{17,25},{24,16},{25,17},{2,10},{3,... | collective-permute-start | bytes 73736 | tf_op jit(solution)/shard_map/ppermute | solution.py:359
  0.0 1.4 %copy-start.4 = (bf16[24,8,64]{2,1,0:T(8,128)(2,1)S(1)}, bf16[24,8,64]{2,1,0:T(8,128)(2,1)}, u32[]{:S(2)}) copy-start(bf16[24,8,64]{2,1,0:T(8,128)(2,1)} %param.11) | copy-start | bytes 73732
  0.0 6.5 %collective-permute-start.3 = (bf16[24,8,256]{2,1,0:T(8,128)(2,1)}, bf16[24,8,256]{2,1,0:T(8,128)(2,1)S(1)}, u32[]{:S(2)}, u32[]{:S(2)}) collective-permute-start(bf16[24,8,256]{2,1,0:T(8,128)(2,1)} %bitcast.7), channel_id=1, source_target_pairs={{0,1},{1,0},{8,9},{9,8},{16,17},{17,16},{24,25},{25,24},{2,3},{3,2... | collective-permute-start | bytes 294920 | tf_op jit(solution)/shard_map/ppermute | solution.py:359
  1.4 2.3 %copy-start.1 = (f32[24,9,3]{0,2,1:T(4,128)S(1)}, f32[24,9,3]{0,2,1:T(4,128)}, u32[]{:S(2)}) copy-start(f32[24,9,3]{0,2,1:T(4,128)} %param.16) | copy-start | bytes 7780
  1.4 2.3 %copy-start.3 = (s32[24,9]{0,1:T(8,128)S(1)}, s32[24,9]{0,1:T(8,128)}, u32[]{:S(2)}) copy-start(s32[24,9]{0,1:T(8,128)} %param.15) | copy-start | bytes 2596
  1.5 2.3 %copy-start.2 = (s32[24,9]{0,1:T(8,128)S(1)}, s32[24,9]{0,1:T(8,128)}, u32[]{:S(2)}) copy-start(s32[24,9]{0,1:T(8,128)} %param.14) | copy-start | bytes 2596
  1.6 5.0 %collective-permute-start.2 = (bf16[25,8,128]{2,1,0:T(8,128)(2,1)S(1)}, bf16[25,8,128]{2,1,0:T(8,128)(2,1)S(1)}, u32[]{:S(2)}, u32[]{:S(2)}) collective-permute-start(bf16[25,8,128]{2,1,0:T(8,128)(2,1)S(1)} %fusion.2.chip_ref), channel_id=1, source_target_pairs={{0,1},{1,0},{8,25},{9,24},{16,17},{17,16},{24,9},{25,8},{2,3},{3,2... | collective-permute-start | bytes 153608 | tf_op jit(solution)/shard_map/ppermute | solution.py:359
  2.3 4.5 %collective-permute-start.1 = (bf16[25,8,128]{2,1,0:T(8,128)(2,1)S(1)}, bf16[25,8,128]{2,1,0:T(8,128)(2,1)S(1)}, u32[]{:S(2)}, u32[]{:S(2)}) collective-permute-start(bf16[25,8,128]{2,1,0:T(8,128)(2,1)S(1)} %fusion.2.chip_ref), channel_id=1, source_target_pairs={{0,16},{1,17},{8,24},{9,25},{16,0},{17,1},{24,8},{25,9},{2,18},{3,... | collective-permute-start | bytes 153608 | tf_op jit(solution)/shard_map/ppermute | solution.py:359
  5.4 2.4 %copy-start = (bf16[1,24,8,256]{3,2,1,0:T(8,128)(2,1)S(1)}, bf16[1,24,8,256]{3,2,1,0:T(8,128)(2,1)}, u32[]{:S(2)}) copy-start(bf16[1,24,8,256]{3,2,1,0:T(8,128)(2,1)} %param.12) | copy-start | bytes 294916
  6.5 1.3 %collective-permute-start.4 = (bf16[24,8,128]{2,1,0:T(8,128)(2,1)S(1)}, bf16[24,8,128]{2,1,0:T(8,128)(2,1)S(1)}, u32[]{:S(2)}, u32[]{:S(2)}) collective-permute-start(bf16[24,8,128]{2,1,0:T(8,128)(2,1)S(1)} %slice.3.sent_ref), channel_id=1, source_target_pairs={{0,8},{1,9},{8,0},{9,1},{16,24},{17,25},{24,16},{25,17},{2,10},{3,... | collective-permute-start | bytes 147464 | tf_op jit(solution)/shard_map/ppermute | solution.py:359
  8.1 3.9 %collective-permute-start.5 = (bf16[112,128]{1,0:T(8,128)(2,1)S(1)}, bf16[112,128]{1,0:T(8,128)(2,1)S(1)}, u32[]{:S(2)}, u32[]{:S(2)}) collective-permute-start(bf16[112,128]{1,0:T(8,128)(2,1)S(1)} %get-tuple-element.37), channel_id=1, source_target_pairs={{0,2},{2,0},{4,6},{6,4},{8,10},{10,8},{12,14},{14,12},{16,18},{18,... | collective-permute-start | bytes 86024 | tf_op jit(solution)/shard_map/ppermute | solution.py:418
  9.7 3.9 %collective-permute-start.6 = (bf16[112,128]{1,0:T(8,128)(2,1)S(1)}, bf16[112,128]{1,0:T(8,128)(2,1)S(1)}, u32[]{:S(2)}, u32[]{:S(2)}) collective-permute-start(bf16[112,128]{1,0:T(8,128)(2,1)S(1)} %get-tuple-element.38), channel_id=1, source_target_pairs={{0,8},{2,4},{4,2},{6,14},{8,0},{10,12},{12,10},{14,6},{16,24},{18,... | collective-permute-start | bytes 86024 | tf_op jit(solution)/shard_map/ppermute | solution.py:418

commit v2 on v1

--- a/solution.py
+++ b/solution.py
@@ -205,20 +205,26 @@
     return mix.reshape(count, B, 16, width)
 
 
-def cell_block(before, mix, w_disco_ref, gain_ref, w_up_ref, bias_ref, w_down_ref):
-    f32, bf16 = jnp.float32, jnp.bfloat16
-    width = before.shape[1]
-    inner = before + jnp.dot(
-        mix, w_disco_ref[...].reshape(B * width, width), preferred_element_type=f32
-    )
+def product(left, right_ref, pieces):
+    wide = right_ref.shape[1] // pieces
+    return jnp.concatenate(
+        [
+            jnp.dot(left, right_ref[:, pl.ds(i * wide, wide)], preferred_element_type=jnp.float32)
+            for i in range(pieces)
+        ],
+        axis=1,
+    )
+
+
+def cell_block(before, mix, w_disco_ref, gain_ref, w_up_ref, bias_ref, w_down_ref, pieces=1):
+    bf16 = jnp.bfloat16
+    inner = before + product(mix, w_disco_ref, pieces)
     mean = jnp.mean(inner, axis=1, keepdims=True)
     variance = jnp.mean(inner * inner, axis=1, keepdims=True) - mean * mean
     scale = lax.rsqrt(jnp.maximum(variance, 0.0) + 1e-05)
     normed = ((inner - mean) * scale * gain_ref[...]).astype(bf16)
-    hidden = jax.nn.gelu(
-        jnp.dot(normed, w_up_ref[...], preferred_element_type=f32) + bias_ref[...]
-    ).astype(bf16)
-    return inner + jnp.dot(hidden, w_down_ref[...], preferred_element_type=f32)
+    hidden = jax.nn.gelu(product(normed, w_up_ref, pieces) + bias_ref[...]).astype(bf16)
+    return inner + product(hidden, w_down_ref, pieces)
 
 
 def mixed_rows(low, high, rows, weights_ref, state_ref):
@@ -277,7 +283,7 @@
     rows, cols, width = out_ref.shape
     block = functools.partial(
         cell_block, w_disco_ref=w_disco_ref, gain_ref=gain_ref, w_up_ref=w_up_ref,
-        bias_ref=bias_ref, w_down_ref=w_down_ref,
+        bias_ref=bias_ref, w_down_ref=w_down_ref, pieces=2,
     )
     inner_copy = pltpu.make_async_copy(inner_ref, out_ref.at[pl.ds(2, rows - 4)], sems.at[0])
     inner_copy.start()
@@ -344,6 +350,7 @@
     rows, cols, quarter = analysis.shape
     width = w_in.shape[1]
     noise = noise[0]
+    w_disco = w_disco.reshape(B * width, width)
     bands = lax.axis_size("lat")
     members = lax.axis_size("member")
     line = B * 16

time: 15.8 us -> 15.8 us (level)
  no operation moved by 1% of the time
where the time goes in v2:
time: 15.8 us; the launch traced here: 15.6 us
  Pallas kernels  5.9 us (37%)
  waiting for transfers between devices  5.04 us (32%)
  starting transfers between devices  4.52 us (29%)
    ppermute x5, waiting for transfers between devices, swapped(): return lax.ppermute(block, ('member', 'lon'), pairs)  3.21 us
    ppermute x5, starting transfers between devices, swapped(): return lax.ppermute(block, ('member', 'lon'), pairs)  2.87 us
    pallas_call x1, Pallas kernels, circle_shards(): pl.pallas_call(edge_kernel, out_shape=shape(rows, cols, width), in_specs=...  2.06 us
    pallas_call x1, Pallas kernels, circle_shards(): pl.pallas_call(inner_kernel, out_shape=(shape(64, width), shape(rows - 4,...  2.03 us
    ppermute x2, waiting for transfers between devices, paired(): return lax.ppermute(edge, ('member', 'lat'), pairs)  1.83 us
    ppermute x2, starting transfers between devices, paired(): return lax.ppermute(edge, ('member', 'lat'), pairs)  1.64 us
    pallas_call x1, Pallas kernels, circle_shards(): pl.pallas_call(weights_kernel, out_shape=(shape(rows * line, 128), shape(...  1.58 us
  transfers between devices with their start and end apart: 7, of which 6 were waited for; matrix products, arithmetic and copies ran while one was open for 1% of the time, Pallas kernels for 23%

profile of v2, /device:TPU:20, one launch (start us, length us, event | category | flops | bytes accessed | tf_op | source)
XLA Modules:
  0.0 15.6 jit_solution(7988720383328777033)
XLA Ops:
  0.0 0.0 collective-permute-start
  0.0 0.0 copy-start.4
  0.0 0.6 %collective-permute-start.3 = (bf16[24,8,256]{2,1,0:T(8,128)(2,1)}, bf16[24,8,256]{2,1,0:T(8,128)(2,1)S(1)}, u32[]{:S(2)}, u32[]{:S(2)}) collective-permute-start(bf16[24,8,256]{2,1,0:T(8,128)(2,1)} %bitcast.8), channel_id=1, source_target_pairs={{0,1},{1,0},{8,9},{9,8},{16,17},{17,16},{24,25},{25,24},{2,3},{3,2... | collective-permute-start | bytes 294920 | tf_op jit(solution)/shard_map/ppermute | solution.py:366
  0.6 0.9 %collective-permute-done = bf16[24,8,64]{2,1,0:T(8,128)(2,1)S(1)} collective-permute-done((bf16[24,8,64]{2,1,0:T(8,128)(2,1)}, bf16[24,8,64]{2,1,0:T(8,128)(2,1)S(1)}, u32[]{:S(2)}, u32[]{:S(2)}) %collective-permute-start) | collective-permute-done | bytes 24608 | tf_op jit(solution)/shard_map/ppermute | solution.py:366
  1.4 0.0 copy-done.4
  1.4 0.0 copy-start.1
  1.4 0.0 copy-start.3
  1.4 0.1 fusion.2.chip_ref
  1.5 0.0 copy-start.2
  1.6 0.7 %collective-permute-start.2 = (bf16[25,8,128]{2,1,0:T(8,128)(2,1)S(1)}, bf16[25,8,128]{2,1,0:T(8,128)(2,1)S(1)}, u32[]{:S(2)}, u32[]{:S(2)}) collective-permute-start(bf16[25,8,128]{2,1,0:T(8,128)(2,1)S(1)} %fusion.2.chip_ref), channel_id=1, source_target_pairs={{0,1},{1,0},{8,25},{9,24},{16,17},{17,16},{24,9},{25,8},{2,3},{3,2... | collective-permute-start | bytes 153608 | tf_op jit(solution)/shard_map/ppermute | solution.py:366
  2.3 1.5 %collective-permute-start.1 = (bf16[25,8,128]{2,1,0:T(8,128)(2,1)S(1)}, bf16[25,8,128]{2,1,0:T(8,128)(2,1)S(1)}, u32[]{:S(2)}, u32[]{:S(2)}) collective-permute-start(bf16[25,8,128]{2,1,0:T(8,128)(2,1)S(1)} %fusion.2.chip_ref), channel_id=1, source_target_pairs={{0,16},{1,17},{8,24},{9,25},{16,0},{17,1},{24,8},{25,9},{2,18},{3,... | collective-permute-start | bytes 153608 | tf_op jit(solution)/shard_map/ppermute | solution.py:366
  3.8 0.0 copy-done.1
  3.8 0.0 copy-done.3
  3.8 0.0 copy-done.2
  3.8 1.6 %shard_map.110 = (bf16[1152,128]{1,0:T(8,128)(2,1)S(1)}, bf16[512,256]{1,0:T(8,128)(2,1)S(1)}, bf16[768,256]{1,0:T(8,128)(2,1)S(1)}, bf16[256,512]{1,0:T(8,128)(...) custom-call(s32[9,24]{1,0:T(8,128)S(1)} %bitcast.11, s32[9,24]{1,0:T(8,128)S(1)} %bitcast.12, ...), custom_call_target="tpu_custom_call" | custom-call | flops 4000 | bytes 3000 | tf_op jit(solution)/shard_map/pallas_call | solution.py:381
  5.4 0.0 copy-start
  5.4 1.1 %collective-permute-done.2 = bf16[25,8,128]{2,1,0:T(8,128)(2,1)S(1)} collective-permute-done((bf16[25,8,128]{2,1,0:T(8,128)(2,1)S(1)}, bf16[25,8,128]{2,1,0:T(8,128)(2,1)S(1)}, u32[]{:S(2)}, u32[]{:S(2)}) %collective-permute-start.2) | collective-permute-done | bytes 51232 | tf_op jit(solution)/shard_map/ppermute | solution.py:366
  6.5 0.0 collective-permute-done.3.from_y_ref
  6.5 0.1 collective-permute-start.4
  6.6 0.2 %collective-permute-done.1.x_ref = bf16[25,8,128]{2,1,0:T(8,128)(2,1)S(1)} collective-permute-done((bf16[25,8,128]{2,1,0:T(8,128)(2,1)S(1)}, bf16[25,8,128]{2,1,0:T(8,128)(2,1)S(1)}, u32[]{:S(2)}, u32[]{:S(2)}) %collective-permute-start.1) | collective-permute-done | bytes 51232 | tf_op jit(solution)/shard_map/ppermute | solution.py:366
  6.8 1.0 %collective-permute-done.4.got_ref = bf16[24,8,128]{2,1,0:T(8,128)(2,1)S(1)} collective-permute-done((bf16[24,8,128]{2,1,0:T(8,128)(2,1)S(1)}, bf16[24,8,128]{2,1,0:T(8,128)(2,1)S(1)}, u32[]{:S(2)}, u32[]{:S(2)}) %collective-permute-start.4) | collective-permute-done | bytes 49184 | tf_op jit(solution)/shard_map/ppermute | solution.py:366
  7.8 0.0 copy-done
  7.8 0.2 %shard_map.111 = (bf16[448,256]{1,0:T(8,128)(2,1)S(1)}, bf16[112,128]{1,0:T(8,128)(2,1)S(1)}, bf16[112,128]{1,0:T(8,128)(2,1)S(1)}) custom-call(bf16[25,8,128]{2,1,0:T(8,128)(2,1)S(1)} %fusion.2.chip_ref, bf16[25,8,128]{2,1,0:T(8,128)(2,1)S(1)} %collective-permute-done.1.x_ref, bf16[24,8,128]{2,1,0:T(8,128)(2,1)S(1)} %slice.3.sent_ref, ...), custom_call_target="tpu_custom_call" | custom-call | flops 200000000 | bytes 1000000 | tf_op jit(solution)/shard_map/pallas_call | solution.py:410
  8.1 1.6 %collective-permute-start.5 = (bf16[112,128]{1,0:T(8,128)(2,1)S(1)}, bf16[112,128]{1,0:T(8,128)(2,1)S(1)}, u32[]{:S(2)}, u32[]{:S(2)}) collective-permute-start(bf16[112,128]{1,0:T(8,128)(2,1)S(1)} %get-tuple-element.37), channel_id=1, source_target_pairs={{0,2},{2,0},{4,6},{6,4},{8,10},{10,8},{12,14},{14,12},{16,18},{18,... | collective-permute-start | bytes 86024 | tf_op jit(solution)/shard_map/ppermute | solution.py:425
  9.7 0.0 collective-permute-start.6
  9.7 2.0 %shard_map.112 = (bf16[64,256]{1,0:T(8,128)(2,1)S(1)}, bf16[20,8,256]{2,1,0:T(8,128)(2,1)S(1)}) custom-call(bf16[448,256]{1,0:T(8,128)(2,1)S(1)} %get-tuple-element.29.state_ref, bf16[1152,128]{1,0:T(8,128)(2,1)S(1)} %get-tuple-element.27.weights_ref, bf16[768,256]{1,0:T(8,128)(2,1)S(1)} %get-tuple-element.30.w_disco_ref, ...), custom_call_target="tpu_custom_call" | custom-call | flops 800000000 | bytes 2000000 | tf_op jit(solution)/shard_map/pallas_call | solution.py:428
  11.7 0.3 %collective-permute-done.5.first_ref = bf16[112,128]{1,0:T(8,128)(2,1)S(1)} collective-permute-done((bf16[112,128]{1,0:T(8,128)(2,1)S(1)}, bf16[112,128]{1,0:T(8,128)(2,1)S(1)}, u32[]{:S(2)}, u32[]{:S(2)}) %collective-permute-start.5) | collective-permute-done | bytes 28704 | tf_op jit(solution)/shard_map/ppermute | solution.py:425
  12.0 1.6 %collective-permute-done.6.second_ref = bf16[112,128]{1,0:T(8,128)(2,1)S(1)} collective-permute-done((bf16[112,128]{1,0:T(8,128)(2,1)S(1)}, bf16[112,128]{1,0:T(8,128)(2,1)S(1)}, u32[]{:S(2)}, u32[]{:S(2)}) %collective-permute-start.6) | collective-permute-done | bytes 28704 | tf_op jit(solution)/shard_map/ppermute | solution.py:425
  13.6 2.1 %shard_map.113 = bf16[24,8,256]{2,1,0:T(8,128)(2,1)} custom-call(bf16[448,256]{1,0:T(8,128)(2,1)S(1)} %get-tuple-element.29.state_ref, bf16[64,256]{1,0:T(8,128)(2,1)S(1)} %get-tuple-element.35.near_ref, bf16[20,8,256]{2,1,0:T(8,128)(2,1)S(1)} %get-tuple-element.36.inner_ref, bf16[112,128]{1,0:T(8,128)(2,1)S(1)} %collective-permute-done.5.first_ref, ...), custom_call_target="tpu_custom_call" | custom-call | flops 100000000 | bytes 2000000 | tf_op jit(solution)/shard_map/pallas_call | solution.py:443
  (2 shorter events, 0.0 us)
Async XLA Ops:
  0.0 1.4 %collective-permute-start = (bf16[24,8,64]{2,1,0:T(8,128)(2,1)}, bf16[24,8,64]{2,1,0:T(8,128)(2,1)S(1)}, u32[]{:S(2)}, u32[]{:S(2)}) collective-permute-start(bf16[24,8,64]{2,1,0:T(8,128)(2,1)} %param.11), channel_id=1, source_target_pairs={{0,8},{1,9},{8,0},{9,1},{16,24},{17,25},{24,16},{25,17},{2,10},{3,... | collective-permute-start | bytes 73736 | tf_op jit(solution)/shard_map/ppermute | solution.py:366
  0.0 1.4 %copy-start.4 = (bf16[24,8,64]{2,1,0:T(8,128)(2,1)S(1)}, bf16[24,8,64]{2,1,0:T(8,128)(2,1)}, u32[]{:S(2)}) copy-start(bf16[24,8,64]{2,1,0:T(8,128)(2,1)} %param.11) | copy-start | bytes 73732
  0.0 6.5 %collective-permute-start.3 = (bf16[24,8,256]{2,1,0:T(8,128)(2,1)}, bf16[24,8,256]{2,1,0:T(8,128)(2,1)S(1)}, u32[]{:S(2)}, u32[]{:S(2)}) collective-permute-start(bf16[24,8,256]{2,1,0:T(8,128)(2,1)} %bitcast.8), channel_id=1, source_target_pairs={{0,1},{1,0},{8,9},{9,8},{16,17},{17,16},{24,25},{25,24},{2,3},{3,2... | collective-permute-start | bytes 294920 | tf_op jit(solution)/shard_map/ppermute | solution.py:366
  1.4 2.3 %copy-start.1 = (f32[24,9,3]{0,2,1:T(4,128)S(1)}, f32[24,9,3]{0,2,1:T(4,128)}, u32[]{:S(2)}) copy-start(f32[24,9,3]{0,2,1:T(4,128)} %param.16) | copy-start | bytes 7780
  1.4 2.3 %copy-start.3 = (s32[24,9]{0,1:T(8,128)S(1)}, s32[24,9]{0,1:T(8,128)}, u32[]{:S(2)}) copy-start(s32[24,9]{0,1:T(8,128)} %param.15) | copy-start | bytes 2596
  1.5 2.3 %copy-start.2 = (s32[24,9]{0,1:T(8,128)S(1)}, s32[24,9]{0,1:T(8,128)}, u32[]{:S(2)}) copy-start(s32[24,9]{0,1:T(8,128)} %param.14) | copy-start | bytes 2596
  1.6 5.0 %collective-permute-start.2 = (bf16[25,8,128]{2,1,0:T(8,128)(2,1)S(1)}, bf16[25,8,128]{2,1,0:T(8,128)(2,1)S(1)}, u32[]{:S(2)}, u32[]{:S(2)}) collective-permute-start(bf16[25,8,128]{2,1,0:T(8,128)(2,1)S(1)} %fusion.2.chip_ref), channel_id=1, source_target_pairs={{0,1},{1,0},{8,25},{9,24},{16,17},{17,16},{24,9},{25,8},{2,3},{3,2... | collective-permute-start | bytes 153608 | tf_op jit(solution)/shard_map/ppermute | solution.py:366
  2.3 4.5 %collective-permute-start.1 = (bf16[25,8,128]{2,1,0:T(8,128)(2,1)S(1)}, bf16[25,8,128]{2,1,0:T(8,128)(2,1)S(1)}, u32[]{:S(2)}, u32[]{:S(2)}) collective-permute-start(bf16[25,8,128]{2,1,0:T(8,128)(2,1)S(1)} %fusion.2.chip_ref), channel_id=1, source_target_pairs={{0,16},{1,17},{8,24},{9,25},{16,0},{17,1},{24,8},{25,9},{2,18},{3,... | collective-permute-start | bytes 153608 | tf_op jit(solution)/shard_map/ppermute | solution.py:366
  5.4 2.4 %copy-start = (bf16[1,24,8,256]{3,2,1,0:T(8,128)(2,1)S(1)}, bf16[1,24,8,256]{3,2,1,0:T(8,128)(2,1)}, u32[]{:S(2)}) copy-start(bf16[1,24,8,256]{3,2,1,0:T(8,128)(2,1)} %param.12) | copy-start | bytes 294916
  6.5 1.3 %collective-permute-start.4 = (bf16[24,8,128]{2,1,0:T(8,128)(2,1)S(1)}, bf16[24,8,128]{2,1,0:T(8,128)(2,1)S(1)}, u32[]{:S(2)}, u32[]{:S(2)}) collective-permute-start(bf16[24,8,128]{2,1,0:T(8,128)(2,1)S(1)} %slice.3.sent_ref), channel_id=1, source_target_pairs={{0,8},{1,9},{8,0},{9,1},{16,24},{17,25},{24,16},{25,17},{2,10},{3,... | collective-permute-start | bytes 147464 | tf_op jit(solution)/shard_map/ppermute | solution.py:366
  8.1 3.9 %collective-permute-start.5 = (bf16[112,128]{1,0:T(8,128)(2,1)S(1)}, bf16[112,128]{1,0:T(8,128)(2,1)S(1)}, u32[]{:S(2)}, u32[]{:S(2)}) collective-permute-start(bf16[112,128]{1,0:T(8,128)(2,1)S(1)} %get-tuple-element.37), channel_id=1, source_target_pairs={{0,2},{2,0},{4,6},{6,4},{8,10},{10,8},{12,14},{14,12},{16,18},{18,... | collective-permute-start | bytes 86024 | tf_op jit(solution)/shard_map/ppermute | solution.py:425
  9.7 3.9 %collective-permute-start.6 = (bf16[112,128]{1,0:T(8,128)(2,1)S(1)}, bf16[112,128]{1,0:T(8,128)(2,1)S(1)}, u32[]{:S(2)}, u32[]{:S(2)}) collective-permute-start(bf16[112,128]{1,0:T(8,128)(2,1)S(1)} %get-tuple-element.38), channel_id=1, source_target_pairs={{0,8},{2,4},{4,2},{6,14},{8,0},{10,12},{12,10},{14,6},{16,24},{18,... | collective-permute-start | bytes 86024 | tf_op jit(solution)/shard_map/ppermute | solution.py:425

commit v3 on v1

--- a/solution.py
+++ b/solution.py
@@ -205,20 +205,39 @@
     return mix.reshape(count, B, 16, width)
 
 
-def cell_block(before, mix, w_disco_ref, gain_ref, w_up_ref, bias_ref, w_down_ref):
+def cell_block(
+    before, mix, w_disco_ref, gain_ref, w_up_ref, bias_ref, w_down_ref, gain_up=None, norm_first=True
+):
     f32, bf16 = jnp.float32, jnp.bfloat16
-    width = before.shape[1]
+    count, width = before.shape
     inner = before + jnp.dot(
         mix, w_disco_ref[...].reshape(B * width, width), preferred_element_type=f32
     )
     mean = jnp.mean(inner, axis=1, keepdims=True)
     variance = jnp.mean(inner * inner, axis=1, keepdims=True) - mean * mean
     scale = lax.rsqrt(jnp.maximum(variance, 0.0) + 1e-05)
-    normed = ((inner - mean) * scale * gain_ref[...]).astype(bf16)
-    hidden = jax.nn.gelu(
-        jnp.dot(normed, w_up_ref[...], preferred_element_type=f32) + bias_ref[...]
-    ).astype(bf16)
-    return inner + jnp.dot(hidden, w_down_ref[...], preferred_element_type=f32)
+    if gain_up is None:
+        gain = jnp.broadcast_to(gain_ref[...], (16, width))
+        rounded = gain.astype(bf16).astype(f32)
+        row = lax.broadcasted_iota(jnp.int32, gain.shape, 0)
+        parts = jnp.where(row == 0, rounded, jnp.where(row == 1, gain - rounded, 0.0))
+        normed = (inner - mean) * scale * gain_ref[...]
+        up = jnp.dot(
+            jnp.concatenate([normed.astype(bf16), parts.astype(bf16)], axis=0),
+            w_up_ref[...],
+            preferred_element_type=f32,
+        )
+        gain_up = up[count : count + 1] + up[count + 1 : count + 2]
+        up = up[:count]
+    elif norm_first:
+        normed = (inner - mean) * scale * gain_ref[...]
+        up = jnp.dot(normed.astype(bf16), w_up_ref[...], preferred_element_type=f32)
+    else:
+        scaled = (inner * gain_ref[...]).astype(bf16)
+        up = jnp.dot(scaled, w_up_ref[...], preferred_element_type=f32)
+        up = (up - mean * gain_up) * scale
+    hidden = jax.nn.gelu(up + bias_ref[...]).astype(bf16)
+    return inner + jnp.dot(hidden, w_down_ref[...], preferred_element_type=f32), gain_up
 
 
 def mixed_rows(low, high, rows, weights_ref, state_ref):
@@ -234,7 +253,7 @@
 
 def inner_kernel(
     state_ref, weights_ref, w_disco_ref, gain_ref, w_up_ref, bias_ref, w_down_ref,
-    near_ref, out_ref, next_ref, mix_ref, own_mix_ref,
+    near_ref, out_ref, gain_up_ref, next_ref, mix_ref, own_mix_ref,
 ):
     f32, bf16 = jnp.float32, jnp.bfloat16
     width = state_ref.shape[1]
@@ -249,9 +268,11 @@
         for i in range(low, high):
             for b in range(B):
                 mix_ref[pl.ds((i - 2) * 16, 16), pl.ds(b * width, width)] = mix[i - low, b].astype(bf16)
-    after = block(
+    after, gain_up = block(
         state_ref[pl.ds(48, (rows - 2) * 16), :].astype(f32), mix_ref[...]
-    ).astype(bf16)
+    )
+    after = after.astype(bf16)
+    gain_up_ref[...] = gain_up
     border = jnp.zeros((48, width), bf16)
     next_ref[pl.ds(0, 48), :] = border
     next_ref[pl.ds(48, (rows - 2) * 16), :] = after
@@ -265,44 +286,47 @@
             for b in range(B):
                 own_mix_ref[pl.ds((i - 3) * cols, cols), pl.ds(b * width, width)] = mix[i - low, b, :cols]
     own = next_ref[pl.ds(64, (rows - 4) * 16), :].astype(f32).reshape(rows - 4, 16, width)[:, :cols]
-    result = block(own.reshape((rows - 4) * cols, width), own_mix_ref[...].astype(bf16))
+    result, _ = block(
+        own.reshape((rows - 4) * cols, width), own_mix_ref[...].astype(bf16), gain_up=gain_up
+    )
     out_ref[...] = result.reshape(rows - 4, cols, width).astype(bf16)
 
 
 def edge_kernel(
     state_ref, near_ref, inner_ref, first_ref, second_ref, weights_ref,
-    w_disco_ref, gain_ref, w_up_ref, bias_ref, w_down_ref, out_ref, next_ref, halo_ref, last_ref, sems,
+    w_disco_ref, gain_ref, w_up_ref, bias_ref, w_down_ref, gain_up_ref, out_ref, next_ref, last_ref, sems,
 ):
     f32, bf16 = jnp.float32, jnp.bfloat16
     rows, cols, width = out_ref.shape
     block = functools.partial(
         cell_block, w_disco_ref=w_disco_ref, gain_ref=gain_ref, w_up_ref=w_up_ref,
-        bias_ref=bias_ref, w_down_ref=w_down_ref,
+        bias_ref=bias_ref, w_down_ref=w_down_ref, gain_up=gain_up_ref[...],
+        norm_first=False,
     )
     inner_copy = pltpu.make_async_copy(inner_ref, out_ref.at[pl.ds(2, rows - 4)], sems.at[0])
     inner_copy.start()
     line = B * 16
     even = lax.axis_index("lat") % 2 == 0
-    halo_ref[jnp.where(even, 1, 0)] = first_ref[...]
-    halo_ref[jnp.where(even, 0, 1)] = second_ref[...]
+    first, second = first_ref[...], second_ref[...]
+    top, bottom = jnp.where(even, second, first), jnp.where(even, first, second)
 
     def received(side):
-        return jnp.concatenate([halo_ref[side, :32, :], halo_ref[side, 32:64, :]], axis=1)
+        return jnp.concatenate([side[:32], side[32:64]], axis=1)
 
     def one_row(mix):
         return jnp.concatenate([mix[b] for b in range(B)], axis=1)
 
-    top_state = jnp.concatenate([received(0), state_ref[pl.ds(32, 32), :]], axis=0)
+    top_state = jnp.concatenate([received(top), state_ref[pl.ds(32, 32), :]], axis=0)
     top_mix = mixed(
-        jnp.concatenate([halo_ref[0, 64:, :], weights_ref[pl.ds(0, line), :]], axis=0)[:, :64],
+        jnp.concatenate([top[64:], weights_ref[pl.ds(0, line), :]], axis=0)[:, :64],
         top_state, 2, width,
     )
     bottom_state = jnp.concatenate(
-        [state_ref[pl.ds(rows * 16, 32), :], received(1)], axis=0
+        [state_ref[pl.ds(rows * 16, 32), :], received(bottom)], axis=0
     )
     bottom_mix = mixed(
         jnp.concatenate(
-            [weights_ref[pl.ds((rows - 1) * line, line), :], halo_ref[1, 64:, :]], axis=0
+            [weights_ref[pl.ds((rows - 1) * line, line), :], bottom[64:]], axis=0
         )[:, :64],
         bottom_state, 2, width,
     )
@@ -310,7 +334,7 @@
         [one_row(mix[i]) for mix in (top_mix, bottom_mix) for i in range(2)], axis=0
     ).astype(bf16)
     edge_state = jnp.concatenate([top_state[16:48], bottom_state[16:48]], axis=0)
-    edge = block(edge_state.astype(f32), edge_mix).astype(bf16)
+    edge = block(edge_state.astype(f32), edge_mix)[0].astype(bf16)
     next_ref[...] = jnp.zeros_like(next_ref)
     next_ref[pl.ds(16, 32), :] = edge[:32]
     next_ref[pl.ds(48, 32), :] = near_ref[pl.ds(0, 32), :]
@@ -322,7 +346,7 @@
         for i in range(low, high):
             mixes.append(one_row(mix[i - low, :, :cols]))
             own.append(next_ref[pl.ds((i + 1) * 16, 16), :].astype(f32)[:cols])
-    result = block(jnp.concatenate(own, axis=0), jnp.concatenate(mixes, axis=0).astype(bf16))
+    result, _ = block(jnp.concatenate(own, axis=0), jnp.concatenate(mixes, axis=0).astype(bf16))
     last_ref[...] = result.reshape(4, cols, width).astype(bf16)
     top_copy = pltpu.make_async_copy(
         last_ref.at[pl.ds(0, 2)], out_ref.at[pl.ds(0, 2)], sems.at[1]
@@ -418,11 +442,13 @@
         return lax.ppermute(edge, ("member", "lat"), pairs)
 
     first, second = paired(first, 0), paired(second, 1)
-    near, inner = pl.pallas_call(
+    near, inner, gain_up = pl.pallas_call(
         inner_kernel,
-        out_shape=(shape(64, width), shape(rows - 4, cols, width)),
+        out_shape=(
+            shape(64, width), shape(rows - 4, cols, width), shape(1, w_up.shape[1], dtype=f32)
+        ),
         in_specs=[vmem] * 7,
-        out_specs=(vmem, vmem),
+        out_specs=(vmem,) * 3,
         scratch_shapes=[
             pltpu.VMEM(((rows + 4) * 16, width), bf16),
             pltpu.VMEM(((rows - 2) * 16, B * width), bf16),
@@ -436,11 +462,10 @@
     result = pl.pallas_call(
         edge_kernel,
         out_shape=shape(rows, cols, width),
-        in_specs=[vmem] * 11,
+        in_specs=[vmem] * 12,
         out_specs=pl.BlockSpec(memory_space=pl.ANY),
         scratch_shapes=[
             pltpu.VMEM(((rows + 4) * 16, width), bf16),
-            pltpu.VMEM((2, 64 + line, 128), bf16),
             pltpu.VMEM((4, cols, width), bf16),
             pltpu.SemaphoreType.DMA((3,)),
         ],
@@ -448,7 +473,7 @@
             flops=100_000_000, bytes_accessed=2_000_000, transcendentals=50_000
         ),
         compiler_params=params,
-    )(state, near, inner, first, second, weights, *dense)
+    )(state, near, inner, first, second, weights, *dense, gain_up)
     return result[None]
 
 

time: 15.8 us -> 15.6 us (0.987)
  Pallas kernels: 5.89 us -> 5.7 us
    pallas_call x1, Pallas kernels: 2.06 us -> 1.88 us  [circle_shards(): pl.pallas_call(edge_kernel, out_shape=shape(rows, cols, width), in_specs=...]
where the time goes in v3:
time: 15.6 us; the launch traced here: 15.5 us
  Pallas kernels  5.7 us (37%)
  waiting for transfers between devices  5.05 us (32%)
  starting transfers between devices  4.52 us (29%)
    ppermute x5, waiting for transfers between devices, swapped(): return lax.ppermute(block, ('member', 'lon'), pairs)  3.21 us
    ppermute x5, starting transfers between devices, swapped(): return lax.ppermute(block, ('member', 'lon'), pairs)  2.87 us
    pallas_call x1, Pallas kernels, circle_shards(): pl.pallas_call(inner_kernel, out_shape=(shape(64, width), shape(rows - 4,...  2.02 us
    pallas_call x1, Pallas kernels, circle_shards(): pl.pallas_call(edge_kernel, out_shape=shape(rows, cols, width), in_specs=...  1.88 us
    ppermute x2, waiting for transfers between devices, paired(): return lax.ppermute(edge, ('member', 'lat'), pairs)  1.84 us
    ppermute x2, starting transfers between devices, paired(): return lax.ppermute(edge, ('member', 'lat'), pairs)  1.64 us
    pallas_call x1, Pallas kernels, circle_shards(): pl.pallas_call(weights_kernel, out_shape=(shape(rows * line, 128), shape(...  1.58 us
  transfers between devices with their start and end apart: 7, of which 6 were waited for; matrix products, arithmetic and copies ran while one was open for 1% of the time, Pallas kernels for 23%

profile of v3, /device:TPU:20, one launch (start us, length us, event | category | flops | bytes accessed | tf_op | source)
XLA Modules:
  0.0 15.5 jit_solution(1390803448275664336)
XLA Ops:
  0.0 0.0 collective-permute-start
  0.0 0.0 copy-start.4
  0.0 0.6 %collective-permute-start.3 = (bf16[24,8,256]{2,1,0:T(8,128)(2,1)}, bf16[24,8,256]{2,1,0:T(8,128)(2,1)S(1)}, u32[]{:S(2)}, u32[]{:S(2)}) collective-permute-start(bf16[24,8,256]{2,1,0:T(8,128)(2,1)} %bitcast.7), channel_id=1, source_target_pairs={{0,1},{1,0},{8,9},{9,8},{16,17},{17,16},{24,25},{25,24},{2,3},{3,2... | collective-permute-start | bytes 294920 | tf_op jit(solution)/shard_map/ppermute | solution.py:383
  0.6 0.9 %collective-permute-done = bf16[24,8,64]{2,1,0:T(8,128)(2,1)S(1)} collective-permute-done((bf16[24,8,64]{2,1,0:T(8,128)(2,1)}, bf16[24,8,64]{2,1,0:T(8,128)(2,1)S(1)}, u32[]{:S(2)}, u32[]{:S(2)}) %collective-permute-start) | collective-permute-done | bytes 24608 | tf_op jit(solution)/shard_map/ppermute | solution.py:383
  1.4 0.0 copy-done.4
  1.4 0.0 copy-start.1
  1.4 0.0 copy-start.3
  1.4 0.1 fusion.2.chip_ref
  1.5 0.0 copy-start.2
  1.6 0.7 %collective-permute-start.2 = (bf16[25,8,128]{2,1,0:T(8,128)(2,1)S(1)}, bf16[25,8,128]{2,1,0:T(8,128)(2,1)S(1)}, u32[]{:S(2)}, u32[]{:S(2)}) collective-permute-start(bf16[25,8,128]{2,1,0:T(8,128)(2,1)S(1)} %fusion.2.chip_ref), channel_id=1, source_target_pairs={{0,1},{1,0},{8,25},{9,24},{16,17},{17,16},{24,9},{25,8},{2,3},{3,2... | collective-permute-start | bytes 153608 | tf_op jit(solution)/shard_map/ppermute | solution.py:383
  2.3 1.5 %collective-permute-start.1 = (bf16[25,8,128]{2,1,0:T(8,128)(2,1)S(1)}, bf16[25,8,128]{2,1,0:T(8,128)(2,1)S(1)}, u32[]{:S(2)}, u32[]{:S(2)}) collective-permute-start(bf16[25,8,128]{2,1,0:T(8,128)(2,1)S(1)} %fusion.2.chip_ref), channel_id=1, source_target_pairs={{0,16},{1,17},{8,24},{9,25},{16,0},{17,1},{24,8},{25,9},{2,18},{3,... | collective-permute-start | bytes 153608 | tf_op jit(solution)/shard_map/ppermute | solution.py:383
  3.8 0.0 copy-done.1
  3.8 0.0 copy-done.3
  3.8 0.0 copy-done.2
  3.8 1.6 %shard_map.110 = (bf16[1152,128]{1,0:T(8,128)(2,1)S(1)}, bf16[512,256]{1,0:T(8,128)(2,1)S(1)}, bf16[3,256,256]{2,1,0:T(8,128)(2,1)S(1)}, bf16[256,512]{1,0:T(8,1...) custom-call(s32[9,24]{1,0:T(8,128)S(1)} %bitcast.10, ...), custom_call_target="tpu_custom_call" | custom-call | flops 4000 | bytes 3000 | tf_op jit(solution)/shard_map/pallas_call | solution.py:398
  5.4 0.0 copy-start
  5.4 1.1 %collective-permute-done.2 = bf16[25,8,128]{2,1,0:T(8,128)(2,1)S(1)} collective-permute-done((bf16[25,8,128]{2,1,0:T(8,128)(2,1)S(1)}, bf16[25,8,128]{2,1,0:T(8,128)(2,1)S(1)}, u32[]{:S(2)}, u32[]{:S(2)}) %collective-permute-start.2) | collective-permute-done | bytes 51232 | tf_op jit(solution)/shard_map/ppermute | solution.py:383
  6.5 0.0 collective-permute-done.3.from_y_ref
  6.5 0.1 collective-permute-start.4
  6.6 0.2 %collective-permute-done.1.x_ref = bf16[25,8,128]{2,1,0:T(8,128)(2,1)S(1)} collective-permute-done((bf16[25,8,128]{2,1,0:T(8,128)(2,1)S(1)}, bf16[25,8,128]{2,1,0:T(8,128)(2,1)S(1)}, u32[]{:S(2)}, u32[]{:S(2)}) %collective-permute-start.1) | collective-permute-done | bytes 51232 | tf_op jit(solution)/shard_map/ppermute | solution.py:383
  6.8 1.0 %collective-permute-done.4.got_ref = bf16[24,8,128]{2,1,0:T(8,128)(2,1)S(1)} collective-permute-done((bf16[24,8,128]{2,1,0:T(8,128)(2,1)S(1)}, bf16[24,8,128]{2,1,0:T(8,128)(2,1)S(1)}, u32[]{:S(2)}, u32[]{:S(2)}) %collective-permute-start.4) | collective-permute-done | bytes 49184 | tf_op jit(solution)/shard_map/ppermute | solution.py:383
  7.8 0.0 copy-done
  7.8 0.2 %shard_map.111 = (bf16[448,256]{1,0:T(8,128)(2,1)S(1)}, bf16[112,128]{1,0:T(8,128)(2,1)S(1)}, bf16[112,128]{1,0:T(8,128)(2,1)S(1)}) custom-call(bf16[25,8,128]{2,1,0:T(8,128)(2,1)S(1)} %fusion.2.chip_ref, bf16[25,8,128]{2,1,0:T(8,128)(2,1)S(1)} %collective-permute-done.1.x_ref, bf16[24,8,128]{2,1,0:T(8,128)(2,1)S(1)} %slice.3.sent_ref, ...), custom_call_target="tpu_custom_call" | custom-call | flops 200000000 | bytes 1000000 | tf_op jit(solution)/shard_map/pallas_call | solution.py:427
  8.1 1.6 %collective-permute-start.5 = (bf16[112,128]{1,0:T(8,128)(2,1)S(1)}, bf16[112,128]{1,0:T(8,128)(2,1)S(1)}, u32[]{:S(2)}, u32[]{:S(2)}) collective-permute-start(bf16[112,128]{1,0:T(8,128)(2,1)S(1)} %get-tuple-element.38), channel_id=1, source_target_pairs={{0,2},{2,0},{4,6},{6,4},{8,10},{10,8},{12,14},{14,12},{16,18},{18,... | collective-permute-start | bytes 86024 | tf_op jit(solution)/shard_map/ppermute | solution.py:442
  9.7 0.0 collective-permute-start.6
  9.7 2.0 %shard_map.112 = (bf16[64,256]{1,0:T(8,128)(2,1)S(1)}, bf16[20,8,256]{2,1,0:T(8,128)(2,1)S(1)}, f32[1,512]{1,0:T(1,128)S(1)}) custom-call(bf16[448,256]{1,0:T(8,128)(2,1)S(1)} %get-tuple-element.30.state_ref, bf16[1152,128]{1,0:T(8,128)(2,1)S(1)} %get-tuple-element.28.weights_ref, bf16[3,256,256]{2,1,0:T(8,128)(2,1)S(1)} %get-tuple-element.31.w_disco_ref, ...), custom_call_target="tpu_custom_call" | custom-call | flops 800000000 | bytes 2000000 | tf_op jit(solution)/shard_map/pallas_call | solution.py:445
  11.7 0.3 %collective-permute-done.5.first_ref = bf16[112,128]{1,0:T(8,128)(2,1)S(1)} collective-permute-done((bf16[112,128]{1,0:T(8,128)(2,1)S(1)}, bf16[112,128]{1,0:T(8,128)(2,1)S(1)}, u32[]{:S(2)}, u32[]{:S(2)}) %collective-permute-start.5) | collective-permute-done | bytes 28704 | tf_op jit(solution)/shard_map/ppermute | solution.py:442
  12.0 1.6 %collective-permute-done.6.second_ref = bf16[112,128]{1,0:T(8,128)(2,1)S(1)} collective-permute-done((bf16[112,128]{1,0:T(8,128)(2,1)S(1)}, bf16[112,128]{1,0:T(8,128)(2,1)S(1)}, u32[]{:S(2)}, u32[]{:S(2)}) %collective-permute-start.6) | collective-permute-done | bytes 28704 | tf_op jit(solution)/shard_map/ppermute | solution.py:442
  13.6 1.9 %shard_map.113 = bf16[24,8,256]{2,1,0:T(8,128)(2,1)} custom-call(bf16[448,256]{1,0:T(8,128)(2,1)S(1)} %get-tuple-element.30.state_ref, bf16[64,256]{1,0:T(8,128)(2,1)S(1)} %get-tuple-element.36.near_ref, bf16[20,8,256]{2,1,0:T(8,128)(2,1)S(1)} %get-tuple-element.37.inner_ref, bf16[112,128]{1,0:T(8,128)(2,1)S(1)} %collective-permute-done.5.first_ref, ...), custom_call_target="tpu_custom_call" | custom-call | flops 100000000 | bytes 2000000 | tf_op jit(solution)/shard_map/pallas_call | solution.py:462
  (2 shorter events, 0.0 us)
Async XLA Ops:
  0.0 1.4 %collective-permute-start = (bf16[24,8,64]{2,1,0:T(8,128)(2,1)}, bf16[24,8,64]{2,1,0:T(8,128)(2,1)S(1)}, u32[]{:S(2)}, u32[]{:S(2)}) collective-permute-start(bf16[24,8,64]{2,1,0:T(8,128)(2,1)} %param.11), channel_id=1, source_target_pairs={{0,8},{1,9},{8,0},{9,1},{16,24},{17,25},{24,16},{25,17},{2,10},{3,... | collective-permute-start | bytes 73736 | tf_op jit(solution)/shard_map/ppermute | solution.py:383
  0.0 1.4 %copy-start.4 = (bf16[24,8,64]{2,1,0:T(8,128)(2,1)S(1)}, bf16[24,8,64]{2,1,0:T(8,128)(2,1)}, u32[]{:S(2)}) copy-start(bf16[24,8,64]{2,1,0:T(8,128)(2,1)} %param.11) | copy-start | bytes 73732
  0.0 6.5 %collective-permute-start.3 = (bf16[24,8,256]{2,1,0:T(8,128)(2,1)}, bf16[24,8,256]{2,1,0:T(8,128)(2,1)S(1)}, u32[]{:S(2)}, u32[]{:S(2)}) collective-permute-start(bf16[24,8,256]{2,1,0:T(8,128)(2,1)} %bitcast.7), channel_id=1, source_target_pairs={{0,1},{1,0},{8,9},{9,8},{16,17},{17,16},{24,25},{25,24},{2,3},{3,2... | collective-permute-start | bytes 294920 | tf_op jit(solution)/shard_map/ppermute | solution.py:383
  1.4 2.3 %copy-start.1 = (f32[24,9,3]{0,2,1:T(4,128)S(1)}, f32[24,9,3]{0,2,1:T(4,128)}, u32[]{:S(2)}) copy-start(f32[24,9,3]{0,2,1:T(4,128)} %param.16) | copy-start | bytes 7780
  1.4 2.3 %copy-start.3 = (s32[24,9]{0,1:T(8,128)S(1)}, s32[24,9]{0,1:T(8,128)}, u32[]{:S(2)}) copy-start(s32[24,9]{0,1:T(8,128)} %param.15) | copy-start | bytes 2596
  1.5 2.3 %copy-start.2 = (s32[24,9]{0,1:T(8,128)S(1)}, s32[24,9]{0,1:T(8,128)}, u32[]{:S(2)}) copy-start(s32[24,9]{0,1:T(8,128)} %param.14) | copy-start | bytes 2596
  1.6 5.0 %collective-permute-start.2 = (bf16[25,8,128]{2,1,0:T(8,128)(2,1)S(1)}, bf16[25,8,128]{2,1,0:T(8,128)(2,1)S(1)}, u32[]{:S(2)}, u32[]{:S(2)}) collective-permute-start(bf16[25,8,128]{2,1,0:T(8,128)(2,1)S(1)} %fusion.2.chip_ref), channel_id=1, source_target_pairs={{0,1},{1,0},{8,25},{9,24},{16,17},{17,16},{24,9},{25,8},{2,3},{3,2... | collective-permute-start | bytes 153608 | tf_op jit(solution)/shard_map/ppermute | solution.py:383
  2.3 4.5 %collective-permute-start.1 = (bf16[25,8,128]{2,1,0:T(8,128)(2,1)S(1)}, bf16[25,8,128]{2,1,0:T(8,128)(2,1)S(1)}, u32[]{:S(2)}, u32[]{:S(2)}) collective-permute-start(bf16[25,8,128]{2,1,0:T(8,128)(2,1)S(1)} %fusion.2.chip_ref), channel_id=1, source_target_pairs={{0,16},{1,17},{8,24},{9,25},{16,0},{17,1},{24,8},{25,9},{2,18},{3,... | collective-permute-start | bytes 153608 | tf_op jit(solution)/shard_map/ppermute | solution.py:383
  5.4 2.4 %copy-start = (bf16[1,24,8,256]{3,2,1,0:T(8,128)(2,1)S(1)}, bf16[1,24,8,256]{3,2,1,0:T(8,128)(2,1)}, u32[]{:S(2)}) copy-start(bf16[1,24,8,256]{3,2,1,0:T(8,128)(2,1)} %param.12) | copy-start | bytes 294916
  6.5 1.3 %collective-permute-start.4 = (bf16[24,8,128]{2,1,0:T(8,128)(2,1)S(1)}, bf16[24,8,128]{2,1,0:T(8,128)(2,1)S(1)}, u32[]{:S(2)}, u32[]{:S(2)}) collective-permute-start(bf16[24,8,128]{2,1,0:T(8,128)(2,1)S(1)} %slice.3.sent_ref), channel_id=1, source_target_pairs={{0,8},{1,9},{8,0},{9,1},{16,24},{17,25},{24,16},{25,17},{2,10},{3,... | collective-permute-start | bytes 147464 | tf_op jit(solution)/shard_map/ppermute | solution.py:383
  8.1 3.9 %collective-permute-start.5 = (bf16[112,128]{1,0:T(8,128)(2,1)S(1)}, bf16[112,128]{1,0:T(8,128)(2,1)S(1)}, u32[]{:S(2)}, u32[]{:S(2)}) collective-permute-start(bf16[112,128]{1,0:T(8,128)(2,1)S(1)} %get-tuple-element.38), channel_id=1, source_target_pairs={{0,2},{2,0},{4,6},{6,4},{8,10},{10,8},{12,14},{14,12},{16,18},{18,... | collective-permute-start | bytes 86024 | tf_op jit(solution)/shard_map/ppermute | solution.py:442
  9.7 3.9 %collective-permute-start.6 = (bf16[112,128]{1,0:T(8,128)(2,1)S(1)}, bf16[112,128]{1,0:T(8,128)(2,1)S(1)}, u32[]{:S(2)}, u32[]{:S(2)}) collective-permute-start(bf16[112,128]{1,0:T(8,128)(2,1)S(1)} %get-tuple-element.39), channel_id=1, source_target_pairs={{0,8},{2,4},{4,2},{6,14},{8,0},{10,12},{12,10},{14,6},{16,24},{18,... | collective-permute-start | bytes 86024 | tf_op jit(solution)/shard_map/ppermute | solution.py:442

commit v4 on v3

--- a/solution.py
+++ b/solution.py
@@ -305,6 +305,10 @@
     )
     inner_copy = pltpu.make_async_copy(inner_ref, out_ref.at[pl.ds(2, rows - 4)], sems.at[0])
     inner_copy.start()
+    for start, count in ((0, 16), (80, 48), ((rows - 6) * 16, 80), ((rows + 3) * 16, 16)):
+        next_ref[pl.ds(start, count), :] = jnp.zeros((count, width), bf16)
+    next_ref[pl.ds(48, 32), :] = near_ref[pl.ds(0, 32), :]
+    next_ref[pl.ds((rows - 1) * 16, 32), :] = near_ref[pl.ds(32, 32), :]
     line = B * 16
     even = lax.axis_index("lat") % 2 == 0
     first, second = first_ref[...], second_ref[...]
@@ -335,10 +339,7 @@
     ).astype(bf16)
     edge_state = jnp.concatenate([top_state[16:48], bottom_state[16:48]], axis=0)
     edge = block(edge_state.astype(f32), edge_mix)[0].astype(bf16)
-    next_ref[...] = jnp.zeros_like(next_ref)
     next_ref[pl.ds(16, 32), :] = edge[:32]
-    next_ref[pl.ds(48, 32), :] = near_ref[pl.ds(0, 32), :]
-    next_ref[pl.ds((rows - 1) * 16, 32), :] = near_ref[pl.ds(32, 32), :]
     next_ref[pl.ds((rows + 1) * 16, 32), :] = edge[32:]
     mixes, own = [], []
     for low, high in ((1, 3), (rows - 1, rows), (rows, rows + 1)):

time: 15.6 us -> 15.6 us (level)
  no operation moved by 1% of the time
where the time goes in v4:
time: 15.6 us; the launch traced here: 15.5 us
  Pallas kernels  5.7 us (37%)
  waiting for transfers between devices  5.05 us (32%)
  starting transfers between devices  4.52 us (29%)
    ppermute x5, waiting for transfers between devices, swapped(): return lax.ppermute(block, ('member', 'lon'), pairs)  3.21 us
    ppermute x5, starting transfers between devices, swapped(): return lax.ppermute(block, ('member', 'lon'), pairs)  2.87 us
    pallas_call x1, Pallas kernels, circle_shards(): pl.pallas_call(inner_kernel, out_shape=(shape(64, width), shape(rows - 4,...  2.02 us
    pallas_call x1, Pallas kernels, circle_shards(): pl.pallas_call(edge_kernel, out_shape=shape(rows, cols, width), in_specs=...  1.88 us
    ppermute x2, waiting for transfers between devices, paired(): return lax.ppermute(edge, ('member', 'lat'), pairs)  1.84 us
    ppermute x2, starting transfers between devices, paired(): return lax.ppermute(edge, ('member', 'lat'), pairs)  1.64 us
    pallas_call x1, Pallas kernels, circle_shards(): pl.pallas_call(weights_kernel, out_shape=(shape(rows * line, 128), shape(...  1.58 us
  transfers between devices with their start and end apart: 7, of which 6 were waited for; matrix products, arithmetic and copies ran while one was open for 1% of the time, Pallas kernels for 23%

profile of v4, /device:TPU:20, one launch (start us, length us, event | category | flops | bytes accessed | tf_op | source)
XLA Modules:
  0.0 15.5 jit_solution(1390803448275664336)
XLA Ops:
  0.0 0.0 collective-permute-start
  0.0 0.0 copy-start.4
  0.0 0.6 %collective-permute-start.3 = (bf16[24,8,256]{2,1,0:T(8,128)(2,1)}, bf16[24,8,256]{2,1,0:T(8,128)(2,1)S(1)}, u32[]{:S(2)}, u32[]{:S(2)}) collective-permute-start(bf16[24,8,256]{2,1,0:T(8,128)(2,1)} %bitcast.7), channel_id=1, source_target_pairs={{0,1},{1,0},{8,9},{9,8},{16,17},{17,16},{24,25},{25,24},{2,3},{3,2... | collective-permute-start | bytes 294920 | tf_op jit(solution)/shard_map/ppermute | solution.py:384
  0.6 0.9 %collective-permute-done = bf16[24,8,64]{2,1,0:T(8,128)(2,1)S(1)} collective-permute-done((bf16[24,8,64]{2,1,0:T(8,128)(2,1)}, bf16[24,8,64]{2,1,0:T(8,128)(2,1)S(1)}, u32[]{:S(2)}, u32[]{:S(2)}) %collective-permute-start) | collective-permute-done | bytes 24608 | tf_op jit(solution)/shard_map/ppermute | solution.py:384
  1.4 0.0 copy-done.4
  1.4 0.0 copy-start.1
  1.4 0.0 copy-start.3
  1.4 0.1 fusion.2.chip_ref
  1.5 0.0 copy-start.2
  1.6 0.7 %collective-permute-start.2 = (bf16[25,8,128]{2,1,0:T(8,128)(2,1)S(1)}, bf16[25,8,128]{2,1,0:T(8,128)(2,1)S(1)}, u32[]{:S(2)}, u32[]{:S(2)}) collective-permute-start(bf16[25,8,128]{2,1,0:T(8,128)(2,1)S(1)} %fusion.2.chip_ref), channel_id=1, source_target_pairs={{0,1},{1,0},{8,25},{9,24},{16,17},{17,16},{24,9},{25,8},{2,3},{3,2... | collective-permute-start | bytes 153608 | tf_op jit(solution)/shard_map/ppermute | solution.py:384
  2.3 1.5 %collective-permute-start.1 = (bf16[25,8,128]{2,1,0:T(8,128)(2,1)S(1)}, bf16[25,8,128]{2,1,0:T(8,128)(2,1)S(1)}, u32[]{:S(2)}, u32[]{:S(2)}) collective-permute-start(bf16[25,8,128]{2,1,0:T(8,128)(2,1)S(1)} %fusion.2.chip_ref), channel_id=1, source_target_pairs={{0,16},{1,17},{8,24},{9,25},{16,0},{17,1},{24,8},{25,9},{2,18},{3,... | collective-permute-start | bytes 153608 | tf_op jit(solution)/shard_map/ppermute | solution.py:384
  3.8 0.0 copy-done.1
  3.8 0.0 copy-done.3
  3.8 0.0 copy-done.2
  3.8 1.6 %shard_map.110 = (bf16[1152,128]{1,0:T(8,128)(2,1)S(1)}, bf16[512,256]{1,0:T(8,128)(2,1)S(1)}, bf16[3,256,256]{2,1,0:T(8,128)(2,1)S(1)}, bf16[256,512]{1,0:T(8,1...) custom-call(s32[9,24]{1,0:T(8,128)S(1)} %bitcast.10, ...), custom_call_target="tpu_custom_call" | custom-call | flops 4000 | bytes 3000 | tf_op jit(solution)/shard_map/pallas_call | solution.py:399
  5.4 0.0 copy-start
  5.4 1.1 %collective-permute-done.2 = bf16[25,8,128]{2,1,0:T(8,128)(2,1)S(1)} collective-permute-done((bf16[25,8,128]{2,1,0:T(8,128)(2,1)S(1)}, bf16[25,8,128]{2,1,0:T(8,128)(2,1)S(1)}, u32[]{:S(2)}, u32[]{:S(2)}) %collective-permute-start.2) | collective-permute-done | bytes 51232 | tf_op jit(solution)/shard_map/ppermute | solution.py:384
  6.5 0.0 collective-permute-done.3.from_y_ref
  6.5 0.1 collective-permute-start.4
  6.6 0.2 %collective-permute-done.1.x_ref = bf16[25,8,128]{2,1,0:T(8,128)(2,1)S(1)} collective-permute-done((bf16[25,8,128]{2,1,0:T(8,128)(2,1)S(1)}, bf16[25,8,128]{2,1,0:T(8,128)(2,1)S(1)}, u32[]{:S(2)}, u32[]{:S(2)}) %collective-permute-start.1) | collective-permute-done | bytes 51232 | tf_op jit(solution)/shard_map/ppermute | solution.py:384
  6.8 1.0 %collective-permute-done.4.got_ref = bf16[24,8,128]{2,1,0:T(8,128)(2,1)S(1)} collective-permute-done((bf16[24,8,128]{2,1,0:T(8,128)(2,1)S(1)}, bf16[24,8,128]{2,1,0:T(8,128)(2,1)S(1)}, u32[]{:S(2)}, u32[]{:S(2)}) %collective-permute-start.4) | collective-permute-done | bytes 49184 | tf_op jit(solution)/shard_map/ppermute | solution.py:384
  7.8 0.0 copy-done
  7.8 0.2 %shard_map.111 = (bf16[448,256]{1,0:T(8,128)(2,1)S(1)}, bf16[112,128]{1,0:T(8,128)(2,1)S(1)}, bf16[112,128]{1,0:T(8,128)(2,1)S(1)}) custom-call(bf16[25,8,128]{2,1,0:T(8,128)(2,1)S(1)} %fusion.2.chip_ref, bf16[25,8,128]{2,1,0:T(8,128)(2,1)S(1)} %collective-permute-done.1.x_ref, bf16[24,8,128]{2,1,0:T(8,128)(2,1)S(1)} %slice.3.sent_ref, ...), custom_call_target="tpu_custom_call" | custom-call | flops 200000000 | bytes 1000000 | tf_op jit(solution)/shard_map/pallas_call | solution.py:428
  8.1 1.6 %collective-permute-start.5 = (bf16[112,128]{1,0:T(8,128)(2,1)S(1)}, bf16[112,128]{1,0:T(8,128)(2,1)S(1)}, u32[]{:S(2)}, u32[]{:S(2)}) collective-permute-start(bf16[112,128]{1,0:T(8,128)(2,1)S(1)} %get-tuple-element.38), channel_id=1, source_target_pairs={{0,2},{2,0},{4,6},{6,4},{8,10},{10,8},{12,14},{14,12},{16,18},{18,... | collective-permute-start | bytes 86024 | tf_op jit(solution)/shard_map/ppermute | solution.py:443
  9.7 0.0 collective-permute-start.6
  9.7 2.0 %shard_map.112 = (bf16[64,256]{1,0:T(8,128)(2,1)S(1)}, bf16[20,8,256]{2,1,0:T(8,128)(2,1)S(1)}, f32[1,512]{1,0:T(1,128)S(1)}) custom-call(bf16[448,256]{1,0:T(8,128)(2,1)S(1)} %get-tuple-element.30.state_ref, bf16[1152,128]{1,0:T(8,128)(2,1)S(1)} %get-tuple-element.28.weights_ref, bf16[3,256,256]{2,1,0:T(8,128)(2,1)S(1)} %get-tuple-element.31.w_disco_ref, ...), custom_call_target="tpu_custom_call" | custom-call | flops 800000000 | bytes 2000000 | tf_op jit(solution)/shard_map/pallas_call | solution.py:446
  11.7 0.3 %collective-permute-done.5.first_ref = bf16[112,128]{1,0:T(8,128)(2,1)S(1)} collective-permute-done((bf16[112,128]{1,0:T(8,128)(2,1)S(1)}, bf16[112,128]{1,0:T(8,128)(2,1)S(1)}, u32[]{:S(2)}, u32[]{:S(2)}) %collective-permute-start.5) | collective-permute-done | bytes 28704 | tf_op jit(solution)/shard_map/ppermute | solution.py:443
  12.0 1.6 %collective-permute-done.6.second_ref = bf16[112,128]{1,0:T(8,128)(2,1)S(1)} collective-permute-done((bf16[112,128]{1,0:T(8,128)(2,1)S(1)}, bf16[112,128]{1,0:T(8,128)(2,1)S(1)}, u32[]{:S(2)}, u32[]{:S(2)}) %collective-permute-start.6) | collective-permute-done | bytes 28704 | tf_op jit(solution)/shard_map/ppermute | solution.py:443
  13.6 1.9 %shard_map.113 = bf16[24,8,256]{2,1,0:T(8,128)(2,1)} custom-call(bf16[448,256]{1,0:T(8,128)(2,1)S(1)} %get-tuple-element.30.state_ref, bf16[64,256]{1,0:T(8,128)(2,1)S(1)} %get-tuple-element.36.near_ref, bf16[20,8,256]{2,1,0:T(8,128)(2,1)S(1)} %get-tuple-element.37.inner_ref, bf16[112,128]{1,0:T(8,128)(2,1)S(1)} %collective-permute-done.5.first_ref, ...), custom_call_target="tpu_custom_call" | custom-call | flops 100000000 | bytes 2000000 | tf_op jit(solution)/shard_map/pallas_call | solution.py:463
  (2 shorter events, 0.0 us)
Async XLA Ops:
  0.0 1.4 %collective-permute-start = (bf16[24,8,64]{2,1,0:T(8,128)(2,1)}, bf16[24,8,64]{2,1,0:T(8,128)(2,1)S(1)}, u32[]{:S(2)}, u32[]{:S(2)}) collective-permute-start(bf16[24,8,64]{2,1,0:T(8,128)(2,1)} %param.11), channel_id=1, source_target_pairs={{0,8},{1,9},{8,0},{9,1},{16,24},{17,25},{24,16},{25,17},{2,10},{3,... | collective-permute-start | bytes 73736 | tf_op jit(solution)/shard_map/ppermute | solution.py:384
  0.0 1.4 %copy-start.4 = (bf16[24,8,64]{2,1,0:T(8,128)(2,1)S(1)}, bf16[24,8,64]{2,1,0:T(8,128)(2,1)}, u32[]{:S(2)}) copy-start(bf16[24,8,64]{2,1,0:T(8,128)(2,1)} %param.11) | copy-start | bytes 73732
  0.0 6.5 %collective-permute-start.3 = (bf16[24,8,256]{2,1,0:T(8,128)(2,1)}, bf16[24,8,256]{2,1,0:T(8,128)(2,1)S(1)}, u32[]{:S(2)}, u32[]{:S(2)}) collective-permute-start(bf16[24,8,256]{2,1,0:T(8,128)(2,1)} %bitcast.7), channel_id=1, source_target_pairs={{0,1},{1,0},{8,9},{9,8},{16,17},{17,16},{24,25},{25,24},{2,3},{3,2... | collective-permute-start | bytes 294920 | tf_op jit(solution)/shard_map/ppermute | solution.py:384
  1.4 2.3 %copy-start.1 = (f32[24,9,3]{0,2,1:T(4,128)S(1)}, f32[24,9,3]{0,2,1:T(4,128)}, u32[]{:S(2)}) copy-start(f32[24,9,3]{0,2,1:T(4,128)} %param.16) | copy-start | bytes 7780
  1.4 2.3 %copy-start.3 = (s32[24,9]{0,1:T(8,128)S(1)}, s32[24,9]{0,1:T(8,128)}, u32[]{:S(2)}) copy-start(s32[24,9]{0,1:T(8,128)} %param.15) | copy-start | bytes 2596
  1.5 2.3 %copy-start.2 = (s32[24,9]{0,1:T(8,128)S(1)}, s32[24,9]{0,1:T(8,128)}, u32[]{:S(2)}) copy-start(s32[24,9]{0,1:T(8,128)} %param.14) | copy-start | bytes 2596
  1.6 5.0 %collective-permute-start.2 = (bf16[25,8,128]{2,1,0:T(8,128)(2,1)S(1)}, bf16[25,8,128]{2,1,0:T(8,128)(2,1)S(1)}, u32[]{:S(2)}, u32[]{:S(2)}) collective-permute-start(bf16[25,8,128]{2,1,0:T(8,128)(2,1)S(1)} %fusion.2.chip_ref), channel_id=1, source_target_pairs={{0,1},{1,0},{8,25},{9,24},{16,17},{17,16},{24,9},{25,8},{2,3},{3,2... | collective-permute-start | bytes 153608 | tf_op jit(solution)/shard_map/ppermute | solution.py:384
  2.3 4.5 %collective-permute-start.1 = (bf16[25,8,128]{2,1,0:T(8,128)(2,1)S(1)}, bf16[25,8,128]{2,1,0:T(8,128)(2,1)S(1)}, u32[]{:S(2)}, u32[]{:S(2)}) collective-permute-start(bf16[25,8,128]{2,1,0:T(8,128)(2,1)S(1)} %fusion.2.chip_ref), channel_id=1, source_target_pairs={{0,16},{1,17},{8,24},{9,25},{16,0},{17,1},{24,8},{25,9},{2,18},{3,... | collective-permute-start | bytes 153608 | tf_op jit(solution)/shard_map/ppermute | solution.py:384
  5.4 2.4 %copy-start = (bf16[1,24,8,256]{3,2,1,0:T(8,128)(2,1)S(1)}, bf16[1,24,8,256]{3,2,1,0:T(8,128)(2,1)}, u32[]{:S(2)}) copy-start(bf16[1,24,8,256]{3,2,1,0:T(8,128)(2,1)} %param.12) | copy-start | bytes 294916
  6.5 1.3 %collective-permute-start.4 = (bf16[24,8,128]{2,1,0:T(8,128)(2,1)S(1)}, bf16[24,8,128]{2,1,0:T(8,128)(2,1)S(1)}, u32[]{:S(2)}, u32[]{:S(2)}) collective-permute-start(bf16[24,8,128]{2,1,0:T(8,128)(2,1)S(1)} %slice.3.sent_ref), channel_id=1, source_target_pairs={{0,8},{1,9},{8,0},{9,1},{16,24},{17,25},{24,16},{25,17},{2,10},{3,... | collective-permute-start | bytes 147464 | tf_op jit(solution)/shard_map/ppermute | solution.py:384
  8.1 3.9 %collective-permute-start.5 = (bf16[112,128]{1,0:T(8,128)(2,1)S(1)}, bf16[112,128]{1,0:T(8,128)(2,1)S(1)}, u32[]{:S(2)}, u32[]{:S(2)}) collective-permute-start(bf16[112,128]{1,0:T(8,128)(2,1)S(1)} %get-tuple-element.38), channel_id=1, source_target_pairs={{0,2},{2,0},{4,6},{6,4},{8,10},{10,8},{12,14},{14,12},{16,18},{18,... | collective-permute-start | bytes 86024 | tf_op jit(solution)/shard_map/ppermute | solution.py:443
  9.7 3.9 %collective-permute-start.6 = (bf16[112,128]{1,0:T(8,128)(2,1)S(1)}, bf16[112,128]{1,0:T(8,128)(2,1)S(1)}, u32[]{:S(2)}, u32[]{:S(2)}) collective-permute-start(bf16[112,128]{1,0:T(8,128)(2,1)S(1)} %get-tuple-element.39), channel_id=1, source_target_pairs={{0,8},{2,4},{4,2},{6,14},{8,0},{10,12},{12,10},{14,6},{16,24},{18,... | collective-permute-start | bytes 86024 | tf_op jit(solution)/shard_map/ppermute | solution.py:443
